TPU v7x, 32 devices: a whole 2x2x4 slice. The times are simulated.
32 devices in a mesh: pipe: 4 (over y, x), expert: 8 (over z, core).
Axes of the slice: x: 2, y: 2, z: 4, core: 2. Of those that a mesh axis runs over, the one named last changes fastest.
Arguments:
- grad_rows: bfloat16 [2, 4, 1024, 3584], P(None, 'pipe', 'expert'), may hold values from -0.29882812 to 0.29882812
- expert_ids: int32 [2, 4, 1024, 8], P(None, 'pipe', 'expert'), may hold values from 0 to 7, all different within a row; in each aligned block of 128 rows (0 to 127, 128 to 255, ..., all dimensions but the last counted through in order) at most 128 rows name the same one
- gate_buckets: int32 [2, 4, 1024, 8], P(None, 'pipe', 'expert'), may hold values from 1 to 64
- saved_hidden: bfloat16 [2, 4, 8, 1024, 1280], P(None, 'pipe', 'expert'), may hold values from -6 to 6
Outputs:
- weight_grad: bfloat16 [4, 8, 1280, 3584], P('pipe', 'expert')
Inputs may be any that keep to these rules, and one draw needn't show every extreme that they name: `expert_ids`: in every direction and rank, each aligned block of 128 tokens names each expert in at most 128 routes and some expert in exactly 128; the 8 ids of a token differ.
All inputs are finite; a program needn't handle non-finite values.
Results may differ from a plain program's by a relative error of at most 0.0058.
Values may be sent and summed in bfloat16 or wider, within the bound.
No kernel may reach another device: no remote copies, remote signals or barrier semaphores. Data moves between devices by JAX's collectives and lax.ppermute only.
A program may use at most 128 MiB of HBM per device.

v0:
```python
import jax
import jax.numpy as jnp
from jax import lax
from jax.sharding import PartitionSpec as P


def swapped(shard, axis, distance):
    return lax.ppermute(shard, axis, [(i, i ^ 1 << distance) for i in range(lax.axis_size(axis))])


def build_outbound(token_rows, route_ids, bucket_ids, experts, capacity):
    tok_count, top_count = route_ids.shape
    flat_ids = route_ids.reshape(-1)
    one_hot = (flat_ids[:, None] == jnp.arange(experts, dtype=jnp.int32)[None, :]).astype(jnp.int32)
    earlier = jnp.cumsum(one_hot, axis=0) - one_hot
    position = jnp.sum(earlier * one_hot, axis=1)
    slot_ids = flat_ids * capacity + position
    weighting = bucket_ids.reshape(-1).astype(jnp.float32) / 64.0
    slot_table = (
        slot_ids[:, None] == jnp.arange(experts * capacity, dtype=jnp.int32)[None, :]
    ).astype(jnp.float32)
    slot_table = slot_table * weighting[:, None]
    spread = jnp.sum(slot_table.reshape(tok_count, top_count, experts * capacity), axis=1).astype(
        jnp.bfloat16
    )
    outbound = lax.dot_general(
        spread, token_rows, (((0,), (0,)), ((), ())), preferred_element_type=jnp.float32
    )
    return outbound.astype(jnp.bfloat16).reshape(experts, capacity, token_rows.shape[1])


def slot_product(hidden_rows, inbound):
    width = inbound.shape[-1]
    flat_in = inbound.reshape(-1, width)
    product = lax.dot_general(
        hidden_rows, flat_in, (((0,), (0,)), ((), ())), preferred_element_type=jnp.float32
    )
    return product.astype(jnp.bfloat16)


def on_device(grad_rows, expert_ids, gate_buckets, saved_hidden):
    experts = lax.axis_size("expert")
    capacity = saved_hidden.shape[3] // experts
    token_rows = grad_rows[:, 0]
    route_ids = expert_ids[:, 0]
    bucket_ids = gate_buckets[:, 0]
    hidden_rows = saved_hidden[:, 0, 0]
    bit_count = lax.axis_size("pipe").bit_length() - 1
    local_batch = (token_rows[0], route_ids[0], bucket_ids[0], hidden_rows[0])
    other_rows = token_rows[1]
    other_hidden = hidden_rows[1]
    other_ids = route_ids[1]
    other_buckets = bucket_ids[1]
    batches = [local_batch, (other_rows, other_ids, other_buckets, other_hidden)]
    send_list = [
        build_outbound(batch[0], batch[1], batch[2], experts, capacity) for batch in batches
    ]
    arrived = (
        lax.all_to_all(send_list[0], "expert", split_axis=0, concat_axis=0, tiled=True),
        lax.all_to_all(send_list[1], "expert", split_axis=0, concat_axis=0, tiled=True),
    )
    partials = [slot_product(batches[index][3], arrived[index]) for index in range(2)]
    mirrored = partials[1]
    for bit_index in range(bit_count):
        mirrored = swapped(mirrored, "pipe", bit_index)
    total_grad = partials[0].astype(jnp.float32) + mirrored.astype(jnp.float32)
    return total_grad.astype(jnp.bfloat16)[None, None]


def solution(mesh):
    return jax.shard_map(
        on_device,
        mesh=mesh,
        in_specs=(
            P(None, "pipe", "expert", None),
            P(None, "pipe", "expert", None),
            P(None, "pipe", "expert", None),
            P(None, "pipe", "expert", None, None),
        ),
        out_specs=P("pipe", "expert", None, None),
        check_vma=False,
    )
```

profile of v0, /device:TPU:0, one launch (start us, length us, event | category | flops | bytes accessed | tf_op | source)
XLA Modules:
  0.0 607.7 jit_solution(42477322324225128)
XLA Ops:
  0.0 0.7 fusion.21
  0.7 0.1 copy.21
  1.0 2.3 reduce-window.16
  3.3 0.3 slice_reduce_fusion
  3.6 0.2 reduce-window.19
  3.9 0.7 multiply_bitcast_fusion.1
  4.7 0.1 copy.18
  4.8 1.4 select_reduce_fusion
  6.1 3.4 convolution_convert_fusion.2
  9.6 167.9 %all_to_all.10 = bf16[8,128,3584]{2,1,0:T(8,128)(2,1)S(1)} all-to-all(bf16[8,128,3584]{2,1,0:T(8,128)(2,1)S(1)} %bitcast.85), channel_id=1, replica_groups=mesh['pipe'=4,'expert'=8] {'expert'}, dimensions={0} | all-to-all | bytes 14680064 | tf_op jit(solution)/shard_map/all_to_all | solution.py:60
  177.5 11.9 %fusion.1 = bf16[1280,3584]{0,1:T(8,128)(2,1)} fusion(bf16[1024,3584]{1,0:T(8,128)(2,1)S(1)} %bitcast.86, bf16[2,1,1,1024,1280]{4,3,2,1,0:T(8,128)(2,1)S(1)} %bitcast.90), kind=kOutput, calls=%fused_computation.4 | convolution fusion | flops 9399828480 | bytes 19136512 | tf_op jit(solution)/shard_map/dot_general | solution.py:35
  189.4 1.5 collective-permute-start
  191.2 2.3 reduce-window.14
  193.5 0.3 slice_reduce_fusion.1
  193.8 0.2 reduce-window.15
  194.2 1.3 select_reduce_fusion.1
  195.6 5.1 convolution_convert_fusion.3
  200.6 5.0 all-to-all-start
  205.7 182.7 %collective-permute-done = bf16[1280,3584]{0,1:T(8,128)(2,1)} collective-permute-done((bf16[1280,3584]{0,1:T(8,128)(2,1)}, bf16[1280,3584]{0,1:T(8,128)(2,1)}, u32[]{:S(2)}, u32[]{:S(2)}) %collective-permute-start) | collective-permute-done | bytes 9175072 | tf_op jit(solution)/shard_map/ppermute | solution.py:8
  388.4 1.5 collective-permute-start.1
  389.9 12.8 %convolution_convert_fusion.1 = bf16[3584,1280]{1,0:T(8,128)(2,1)S(1)} fusion(bf16[1024,3584]{1,0:T(8,128)(2,1)} %bitcast.5, bf16[2,1,1,1024,1280]{4,3,2,1,0:T(8,128)(2,1)} %param.7), kind=kOutput, calls=%fused_computation.3 | convolution fusion | flops 9399828480 | bytes 19136512 | tf_op jit(solution)/shard_map/dot_general | solution.py:35
  402.8 183.7 %collective-permute-done.1 = bf16[1280,3584]{0,1:T(8,128)(2,1)} collective-permute-done((bf16[1280,3584]{0,1:T(8,128)(2,1)}, bf16[1280,3584]{0,1:T(8,128)(2,1)}, u32[]{:S(2)}, u32[]{:S(2)}) %collective-permute-start.1) | collective-permute-done | bytes 9175072 | tf_op jit(solution)/shard_map/ppermute | solution.py:8
  586.5 8.5 %fusion.2 = bf16[1,1,1280,3584]{2,3,1,0:T(8,128)(2,1)} fusion(bf16[1280,3584]{0,1:T(8,128)(2,1)} %collective-permute-done.1, bf16[3584,1280]{1,0:T(8,128)(2,1)S(1)} %convolution_convert_fusion.1), kind=kLoop, calls=%fused_computation.5 | loop fusion | flops 18350080 | bytes 27525120 | tf_op jit(solution)/shard_map/broadcast_in_dim | solution.py:67
  595.0 12.7 %copy.19 = bf16[1,1,1280,3584]{3,2,1,0:T(8,128)(2,1)} copy(bf16[1,1,1280,3584]{2,3,1,0:T(8,128)(2,1)} %fusion.2) | data formatting | bytes 18350080 | tf_op jit(solution)/shard_map/broadcast_in_dim | solution.py:67
  (24 shorter events, 1.0 us)
Async XLA Ops:
  6.1 171.3 %slice-start = ((s8[5242880]{0:T(1024)(128)(4,1)}), s8[4194304]{0:T(1024)(128)(4,1)S(1)}, s32[]{:S(2)}) async-start(s8[5242880]{0:T(1024)(128)(4,1)} %bitcast.89), calls=%async_computation.2 | async-start | bytes 8388608
  9.6 167.9 %slice-start.1 = ((s8[5242880]{0:T(1024)(128)(4,1)}), s8[1048576]{0:T(1024)(128)(4,1)S(1)}, s32[]{:S(2)}) async-start(s8[5242880]{0:T(1024)(128)(4,1)} %bitcast.89), calls=%async_computation.3 | async-start | bytes 2097152
  177.5 18.1 %copy-start = (bf16[2,1,128,3584]{3,2,1,0:T(8,128)(2,1)S(1)}, bf16[2,1,128,3584]{3,2,1,0:T(8,128)(2,1)}, u32[]{:S(2)}) copy-start(bf16[2,1,128,3584]{3,2,1,0:T(8,128)(2,1)} %param.4) | copy-start | bytes 5505028
  189.4 199.0 %collective-permute-start = (bf16[1280,3584]{0,1:T(8,128)(2,1)}, bf16[1280,3584]{0,1:T(8,128)(2,1)}, u32[]{:S(2)}, u32[]{:S(2)}) collective-permute-start(bf16[1280,3584]{0,1:T(8,128)(2,1)} %fusion.1), channel_id=1, source_target_pairs={{0,8},{8,0},{16,24},{24,16},{1,9},{9,1},{17,25},{25,17},{2,10},{10... | collective-permute-start | bytes 27525128 | tf_op jit(solution)/shard_map/ppermute | solution.py:8
  200.6 189.3 %all-to-all-start = ((bf16[8,128,3584]{2,1,0:T(8,128)(2,1)}), bf16[8,128,3584]{2,1,0:T(8,128)(2,1)}, u32[]{:S(2)}, u32[]{:S(2)}) async-start(bf16[8,128,3584]{2,1,0:T(8,128)(2,1)} %bitcast.84), calls=%async_computation | async-start | bytes 14680064 | tf_op jit(solution)/shard_map/all_to_all | solution.py:59
  388.4 198.1 %collective-permute-start.1 = (bf16[1280,3584]{0,1:T(8,128)(2,1)}, bf16[1280,3584]{0,1:T(8,128)(2,1)}, u32[]{:S(2)}, u32[]{:S(2)}) collective-permute-start(bf16[1280,3584]{0,1:T(8,128)(2,1)} %collective-permute-done), channel_id=1, source_target_pairs={{0,16},{8,24},{16,0},{24,8},{1,17},{9,25},{17,1},{25,9},{2,18},{10... | collective-permute-start | bytes 27525128 | tf_op jit(solution)/shard_map/ppermute | solution.py:8
where the time goes:
time: 608 us
  waiting for transfers between devices  366 us (60%)
  blocking collectives  168 us (28%)
  matrix products  33.3 us (5%)
  other arithmetic  17 us (3%)
  local copies, waits for them, and re-layouts  15 us (2%)
  starting transfers between devices  8.02 us (1%)
    ppermute x2, waiting for transfers between devices, swapped(): lax.ppermute(shard, axis, [(i, i ^ 1 << distance) for i in range(lax.axis...  366 us
    all_to_all x1, blocking collectives, on_device(): lax.all_to_all(send_list[1], 'expert', split_axis=0, concat_axis=0, tiled...  168 us
    dot_general x2, matrix products, slot_product(): lax.dot_general(hidden_rows, flat_in, (((0,), (0,)), ((), ())), preferred...  24.8 us
    broadcast_in_dim x1, local copies, waits for them, and re-layouts, on_device(): return total_grad.astype(jnp.bfloat16)[None, None]  12.7 us
  transfers between devices with their start and end apart: 3, of which 2 were waited for; matrix products, arithmetic and copies ran while one was open for 4% of the time, Pallas kernels for 0%

commit v1 on v0

v1 whole, which is shorter than its diff:
```python
import functools
import jax
import jax.numpy as jnp
from jax import lax
from jax.experimental import pallas as pl
from jax.experimental.pallas import tpu as pltpu
from jax.sharding import PartitionSpec as P

BF16 = jnp.bfloat16
F32 = jnp.float32
TILE = 256


def mirror(shard):
    ranks = lax.axis_size("pipe")
    return lax.ppermute(shard, "pipe", [(i, ranks - 1 - i) for i in range(ranks)])


def core_swap(shard):
    count = lax.axis_size("expert")
    return lax.ppermute(shard, "expert", [(i, i ^ 1) for i in range(count)])


def chip_shift(shard):
    count = lax.axis_size("expert")
    return lax.ppermute(shard, "expert", [(i, (i + 2) % count) for i in range(count)])


def after(value, *earlier):
    return lax.optimization_barrier((value,) + earlier)[0]


def build_outbound(token_rows, route_ids, bucket_ids, experts, capacity):
    tok_count, top_count = route_ids.shape
    flat_ids = route_ids.reshape(-1)
    one_hot = (flat_ids[:, None] == jnp.arange(experts, dtype=jnp.int32)[None, :]).astype(jnp.int32)
    earlier = jnp.cumsum(one_hot, axis=0) - one_hot
    position = jnp.sum(earlier * one_hot, axis=1)
    slot_ids = flat_ids * capacity + position
    weighting = bucket_ids.reshape(-1).astype(F32) / 64.0
    slot_table = (
        slot_ids[:, None] == jnp.arange(experts * capacity, dtype=jnp.int32)[None, :]
    ).astype(F32)
    slot_table = slot_table * weighting[:, None]
    spread = jnp.sum(slot_table.reshape(tok_count, top_count, experts * capacity), axis=1).astype(BF16)
    outbound = lax.dot_general(
        spread, token_rows, (((0,), (0,)), ((), ())), preferred_element_type=F32
    )
    return outbound.astype(BF16).reshape(experts, capacity, token_rows.shape[1])


def slot_product(hidden_rows, inbound):
    flat_in = inbound.reshape(-1, inbound.shape[-1])
    product = lax.dot_general(
        hidden_rows, flat_in, (((0,), (0,)), ((), ())), preferred_element_type=F32
    )
    return product.astype(BF16)


def routed(token_rows, route_ids, bucket_ids, hidden_rows, experts, capacity):
    partials = []
    for index in range(2):
        outbound = build_outbound(
            token_rows[index], route_ids[index], bucket_ids[index], experts, capacity
        )
        arrived = lax.all_to_all(outbound, "expert", split_axis=0, concat_axis=0, tiled=True)
        partials.append(slot_product(hidden_rows[index], arrived))
    return (partials[0].astype(F32) + mirror(partials[1]).astype(F32)).astype(BF16)


def scale_kernel(order_ref, hidden_ref, gate_ref, out_ref):
    turned = hidden_ref[...].astype(F32).T
    out_ref[...] = (turned * gate_ref[0]).astype(BF16)


def scaled_transposed(order, hidden, gates):
    blocks, _, rows = gates.shape
    width = hidden.shape[1]
    return pl.pallas_call(
        scale_kernel,
        grid_spec=pltpu.PrefetchScalarGridSpec(
            num_scalar_prefetch=1,
            grid=(blocks,),
            in_specs=[
                pl.BlockSpec((rows, width), lambda i, order: (order[i], 0)),
                pl.BlockSpec((1, 1, rows), lambda i, order: (order[i], 0, 0)),
            ],
            out_specs=pl.BlockSpec((width, rows), lambda i, order: (0, i)),
        ),
        out_shape=jax.ShapeDtypeStruct((width, blocks * rows), BF16),
        compiler_params=pltpu.CompilerParams(vmem_limit_bytes=16 << 20),
        cost_estimate=pl.CostEstimate(
            flops=hidden.size, bytes_accessed=4 * hidden.size, transcendentals=0
        ),
        name="scale_hidden",
    )(order, hidden, gates)


def product_kernel(count, add, hidden_ref, *refs):
    rows = jnp.concatenate([ref[...] for ref in refs[:count]], axis=0)
    product = jnp.dot(hidden_ref[...], rows, preferred_element_type=F32)
    if add:
        product = product + refs[count][...].astype(F32)
    refs[-1][...] = product.astype(BF16)


def block_product(hidden, pieces, total, column, width, add):
    out_rows, depth = hidden.shape
    chunk = pieces[0].shape[1]
    first = column // TILE
    in_specs = [pl.BlockSpec((out_rows, depth), lambda j: (0, 0))]
    in_specs += [pl.BlockSpec((p.shape[0], TILE), lambda j: (0, j)) for p in pieces]
    operands = [hidden, *pieces]
    aliases = {}
    out_spec = pl.BlockSpec((out_rows, TILE), lambda j: (0, first + j))
    if total is not None:
        in_specs.append(out_spec if add else pl.BlockSpec(memory_space=pl.ANY))
        aliases = {len(operands): 0}
        operands.append(total)
    return pl.pallas_call(
        functools.partial(product_kernel, len(pieces), add),
        grid=(chunk // TILE,),
        in_specs=in_specs,
        out_specs=out_spec,
        out_shape=jax.ShapeDtypeStruct((out_rows, width), BF16),
        input_output_aliases=aliases,
        compiler_params=pltpu.CompilerParams(vmem_limit_bytes=32 << 20),
        cost_estimate=pl.CostEstimate(
            flops=2 * out_rows * depth * chunk,
            bytes_accessed=2 * (out_rows * depth + depth * chunk + 2 * out_rows * chunk),
            transcendentals=0,
        ),
        name="block_product",
    )(*operands)


def gathered(token_rows, route_ids, bucket_ids, hidden_rows, experts):
    width = token_rows.shape[2]
    steps = experts // 2
    me = lax.axis_index("expert")
    rank = lax.axis_index("pipe")
    ranks = lax.axis_size("pipe")
    order = jnp.stack(
        [2 * lax.rem(me // 2 + steps - i // 2, steps) + (me % 2 ^ i % 2) for i in range(experts)]
    ).astype(jnp.int32)

    named = route_ids[:, None] == jnp.arange(experts, dtype=jnp.int32)[None, :, None, None]
    gates = jnp.sum(jnp.where(named, bucket_ids[:, None], 0), axis=3).astype(F32) / 64.0
    all_gates = lax.all_gather(gates, ("pipe", "expert"), axis=0, tiled=False)
    all_gates = all_gates.reshape((ranks, experts) + gates.shape)
    all_gates = lax.dynamic_index_in_dim(all_gates, me, axis=3, keepdims=True)
    gates_0 = lax.dynamic_index_in_dim(all_gates[:, :, 0], rank, axis=0, keepdims=False)
    gates_1 = lax.dynamic_index_in_dim(all_gates[:, :, 1], ranks - 1 - rank, axis=0, keepdims=False)

    cut = (width // 2) // TILE * TILE
    spans = [(0, cut), (cut, width)]
    rows_1 = mirror(token_rows[1])
    hidden_1 = mirror(hidden_rows[1])
    sent = []
    pieces = [[[] for _ in spans] for _ in range(2)]
    for direction, source in enumerate((token_rows[0], rows_1)):
        if direction == 1:
            source = after(source, sent[-3])
        held = [source[:, lo:hi] for lo, hi in spans]
        for step in range(steps):
            for index in range(len(spans)):
                block = held[index]
                pieces[direction][index] += [block, core_swap(block)]
                if step < steps - 1:
                    held[index] = chip_shift(block)
                    sent.append(held[index])

    scaled_0 = scaled_transposed(order, hidden_rows[0], gates_0)
    scaled_1 = scaled_transposed(order, hidden_1, gates_1)
    total = None
    for index, (lo, _) in enumerate(spans):
        total = block_product(scaled_0, pieces[0][index], total, lo, width, False)
    for index, (lo, _) in enumerate(spans):
        total = block_product(scaled_1, pieces[1][index], total, lo, width, True)
    return total


def on_device(grad_rows, expert_ids, gate_buckets, saved_hidden):
    experts = lax.axis_size("expert")
    capacity = saved_hidden.shape[3] // experts
    tok_count, top_count = expert_ids.shape[2:]
    token_rows, route_ids, bucket_ids = grad_rows[:, 0], expert_ids[:, 0], gate_buckets[:, 0]
    hidden_rows = saved_hidden[:, 0, 0]
    if top_count == experts and capacity == tok_count and experts % 2 == 0:
        result = gathered(token_rows, route_ids, bucket_ids, hidden_rows, experts)
    else:
        result = routed(token_rows, route_ids, bucket_ids, hidden_rows, experts, capacity)
    return result[None, None]


def solution(mesh):
    return jax.shard_map(
        on_device,
        mesh=mesh,
        in_specs=(
            P(None, "pipe", "expert", None),
            P(None, "pipe", "expert", None),
            P(None, "pipe", "expert", None),
            P(None, "pipe", "expert", None, None),
        ),
        out_specs=P("pipe", "expert", None, None),
        check_vma=False,
    )
```

time: 608 us -> 204 us (0.34)
  waiting for transfers between devices: 366 us -> 82.1 us
  blocking collectives: 168 us -> 49.6 us
  Pallas kernels: 0 us -> 43.9 us
  matrix products: 33.3 us -> 0 us
  other arithmetic: 17 us -> 0.03 us
  starting transfers between devices: 8.02 us -> 18.3 us
  local copies, waits for them, and re-layouts: 15 us -> 8.54 us
    ppermute x2 -> x30, waiting for transfers between devices: 366 us -> 82.1 us  [the longest x12 81.9 us: chip_shift(): lax.ppermute(shard, 'expert', [(i, (i + 2) % count) for i in range(count)])]
    all_to_all x1 -> x0, blocking collectives: 168 us -> none  [on_device(): lax.all_to_all(send_list[1], 'expert', split_axis=0, concat_axis=0, tiled...]
    all_gather x0 -> x1, blocking collectives: none -> 49.6 us  [gathered(): all_gates = lax.all_gather(gates, ('pipe', 'expert'), axis=0, tiled=False)]
    pallas_call x0 -> x6, Pallas kernels: none -> 43.9 us  [the longest x4 35.5 us: block_product(): pl.pallas_call(functools.partial(product_kernel, len(pieces), add), grid=...]
    dot_general x4 -> x0, matrix products: 33.3 us -> none  [the longest x2 24.8 us: slot_product(): lax.dot_general(hidden_rows, flat_in, (((0,), (0,)), ((), ())), preferred...]
    ppermute x2 -> x30, starting transfers between devices: 3.01 us -> 18.3 us  [the longest x12 9.32 us: chip_shift(): lax.ppermute(shard, 'expert', [(i, (i + 2) % count) for i in range(count)])]
    broadcast_in_dim x1 -> x0, local copies, waits for them, and re-layouts: 12.7 us -> none  [on_device(): return total_grad.astype(jnp.bfloat16)[None, None]]
    broadcast_in_dim x1 -> x0, other arithmetic: 8.47 us -> none  [on_device(): return total_grad.astype(jnp.bfloat16)[None, None]]
  transfers between devices with their start and end apart: 3 -> 30, of which waited for: 2 -> 11; matrix products, arithmetic and copies ran while one was open for 4% -> 1% of each run, Pallas kernels for 0% -> 17%
where the time goes in v1:
time: 204 us; the launch traced here: 203 us
  waiting for transfers between devices  82.1 us (40%)
  blocking collectives  49.6 us (24%)
  Pallas kernels  43.9 us (22%)
  starting transfers between devices  18.3 us (9%)
  local copies, waits for them, and re-layouts  8.54 us (4%)
    ppermute x12, waiting for transfers between devices, chip_shift(): lax.ppermute(shard, 'expert', [(i, (i + 2) % count) for i in range(count)])  81.9 us
    all_gather x1, blocking collectives, gathered(): all_gates = lax.all_gather(gates, ('pipe', 'expert'), axis=0, tiled=False)  49.6 us
    pallas_call x4, Pallas kernels, block_product(): pl.pallas_call(functools.partial(product_kernel, len(pieces), add), grid=...  35.5 us
    ppermute x12, starting transfers between devices, chip_shift(): lax.ppermute(shard, 'expert', [(i, (i + 2) % count) for i in range(count)])  9.32 us
    pallas_call x2, Pallas kernels, scaled_transposed(): pl.pallas_call(scale_kernel, grid_spec=pltpu.PrefetchScalarGridSpec(num_s...  8.38 us
    ppermute x2, starting transfers between devices, mirror(): lax.ppermute(shard, 'pipe', [(i, ranks - 1 - i) for i in range(ranks)])  5.43 us
  transfers between devices with their start and end apart: 30, of which 11 were waited for; matrix products, arithmetic and copies ran while one was open for 1% of the time, Pallas kernels for 17%

profile of v1, /device:TPU:0, one launch (start us, length us, event | category | flops | bytes accessed | tf_op | source)
XLA Modules:
  0.0 202.9 jit_solution(12984510281785186950)
XLA Ops:
  0.0 1.7 slice_bitcast_fusion.2
  1.8 3.1 %collective-permute-start.2 = (bf16[128,1792]{1,0:T(8,128)(2,1)S(1)}, bf16[128,1792]{1,0:T(8,128)(2,1)S(1)}, u32[]{:S(2)}, u32[]{:S(2)}) collective-permute-start(bf16[128,1792]{1,0:T(8,128)(2,1)S(1)} %get-tuple-element.12.refs_0_), channel_id=1, source_target_pairs={{0,2},{1,3},{2,4},{3,5},{4,6},{5,7},{6,0},{7,1},{8,10},{9,11},{10,... | collective-permute-start | bytes 1376264 | tf_op jit(solution)/shard_map/ppermute | solution.py:26
  4.9 1.6 collective-permute-start.24
  6.5 11.8 %collective-permute-done.2.refs_2_ = bf16[128,1792]{1,0:T(8,128)(2,1)S(1)} collective-permute-done((bf16[128,1792]{1,0:T(8,128)(2,1)S(1)}, bf16[128,1792]{1,0:T(8,128)(2,1)S(1)}, u32[]{:S(2)}, u32[]{:S(2)}) %collective-permute-start.2) | collective-permute-done | bytes 458784 | tf_op jit(solution)/shard_map/ppermute | solution.py:26
  18.3 2.7 %collective-permute-start.1 = (bf16[128,3584]{1,0:T(8,128)(2,1)S(1)}, bf16[128,3584]{1,0:T(8,128)(2,1)S(1)}, u32[]{:S(2)}, u32[]{:S(2)}) collective-permute-start(bf16[128,3584]{1,0:T(8,128)(2,1)S(1)} %get-tuple-element.10), channel_id=1, source_target_pairs={{0,24},{8,16},{16,8},{24,0},{1,25},{9,17},{17,9},{25,1},{2,26},{10... | collective-permute-start | bytes 2752520 | tf_op jit(solution)/shard_map/ppermute | solution.py:16
  21.5 6.5 %collective-permute-done.24.refs_2_ = bf16[128,1792]{1,0:T(8,128)(2,1)S(1)} collective-permute-done((bf16[128,1792]{1,0:T(8,128)(2,1)S(1)}, bf16[128,1792]{1,0:T(8,128)(2,1)S(1)}, u32[]{:S(2)}, u32[]{:S(2)}) %collective-permute-start.24) | collective-permute-done | bytes 458784 | tf_op jit(solution)/shard_map/ppermute | solution.py:26
  28.1 9.9 %collective-permute-done.3.refs_4_ = bf16[128,1792]{1,0:T(8,128)(2,1)} collective-permute-done((bf16[128,1792]{1,0:T(8,128)(2,1)S(1)}, bf16[128,1792]{1,0:T(8,128)(2,1)}, u32[]{:S(2)}, u32[]{:S(2)}) %collective-permute-start.3) | collective-permute-done | bytes 458784 | tf_op jit(solution)/shard_map/ppermute | solution.py:26
  38.0 1.8 slice_bitcast_fusion
  39.9 2.7 %collective-permute-start = (bf16[1024,1280]{1,0:T(8,128)(2,1)}, bf16[1024,1280]{1,0:T(8,128)(2,1)}, u32[]{:S(2)}, u32[]{:S(2)}) collective-permute-start(bf16[1024,1280]{1,0:T(8,128)(2,1)} %get-tuple-element.8), channel_id=1, source_target_pairs={{0,24},{8,16},{16,8},{24,0},{1,25},{9,17},{17,9},{25,1},{2,26},{10... | collective-permute-start | bytes 7864328 | tf_op jit(solution)/shard_map/ppermute | solution.py:16
  42.9 4.0 %collective-permute-done.26.refs_4_ = bf16[128,1792]{1,0:T(8,128)(2,1)S(1)} collective-permute-done((bf16[128,1792]{1,0:T(8,128)(2,1)S(1)}, bf16[128,1792]{1,0:T(8,128)(2,1)S(1)}, u32[]{:S(2)}, u32[]{:S(2)}) %collective-permute-start.26) | collective-permute-done | bytes 458784 | tf_op jit(solution)/shard_map/ppermute | solution.py:26
  51.5 10.7 %collective-permute-done.28.refs_6_ = bf16[128,1792]{1,0:T(8,128)(2,1)S(1)} collective-permute-done((bf16[128,1792]{1,0:T(8,128)(2,1)S(1)}, bf16[128,1792]{1,0:T(8,128)(2,1)S(1)}, u32[]{:S(2)}, u32[]{:S(2)}) %collective-permute-start.28) | collective-permute-done | bytes 458784 | tf_op jit(solution)/shard_map/ppermute | solution.py:26
  63.5 8.5 %collective-permute-done.21.refs_6_ = bf16[128,1792]{1,0:T(8,128)(2,1)S(1)} collective-permute-done((bf16[128,1792]{1,0:T(8,128)(2,1)}, bf16[128,1792]{1,0:T(8,128)(2,1)S(1)}, u32[]{:S(2)}, u32[]{:S(2)}) %collective-permute-start.21) | collective-permute-done | bytes 458784 | tf_op jit(solution)/shard_map/ppermute | solution.py:26
  72.8 9.1 %collective-permute-done.12.refs_2_ = bf16[128,1792]{1,0:T(8,128)(2,1)} collective-permute-done((bf16[128,1792]{1,0:T(8,128)(2,1)}, bf16[128,1792]{1,0:T(8,128)(2,1)}, u32[]{:S(2)}, u32[]{:S(2)}) %collective-permute-start.12) | collective-permute-done | bytes 458784 | tf_op jit(solution)/shard_map/ppermute | solution.py:26
  82.6 9.2 %collective-permute-done.5.refs_2_ = bf16[128,1792]{1,0:T(8,128)(2,1)} collective-permute-done((bf16[128,1792]{1,0:T(8,128)(2,1)S(1)}, bf16[128,1792]{1,0:T(8,128)(2,1)}, u32[]{:S(2)}, u32[]{:S(2)}) %collective-permute-start.5) | collective-permute-done | bytes 458784 | tf_op jit(solution)/shard_map/ppermute | solution.py:26
  91.8 9.8 %collective-permute-done.14.refs_4_ = bf16[128,1792]{1,0:T(8,128)(2,1)} collective-permute-done((bf16[128,1792]{1,0:T(8,128)(2,1)}, bf16[128,1792]{1,0:T(8,128)(2,1)}, u32[]{:S(2)}, u32[]{:S(2)}) %collective-permute-start.14) | collective-permute-done | bytes 458784 | tf_op jit(solution)/shard_map/ppermute | solution.py:26
  101.6 49.6 %all-gather = f32[64,8,128]{2,1,0:T(8,128)S(1)} all-gather(f32[2,8,128]{2,1,0:T(8,128)S(1)} %convert_multiply_fusion), channel_id=2, replica_groups=mesh['pipe'=4,'expert'=8] {'pipe','expert'}, dimensions={0}, use_global_device_ids=true | all-gather | bytes 270336 | tf_op jit(solution)/shard_map/all_gather | solution.py:149
  153.3 1.8 collective-permute-start.9
  155.3 2.6 %scale_hidden.3.hidden_ref = bf16[1280,1024]{1,0:T(8,128)(2,1)S(1)} custom-call(s32[8]{0:T(128)S(1)} %stack.35.order_ref, bf16[1024,1280]{1,0:T(8,128)(2,1)S(1)} %get-tuple-element.7.hidden_ref, f32[8,1,128]{2,1,0:T(1,128)S(1)} %get-tuple-element.15.gate_ref), custom_call_target="tpu_custom_call" | custom-call | flops 1310720 | bytes 5242880 | tf_op jit(solution)/shard_map/scale_hidden/pallas_call | solution.py:79
  158.1 7.2 %block_product.4.refs_8_ = bf16[1280,3584]{1,0:T(8,128)(2,1)} custom-call(bf16[1280,1024]{1,0:T(8,128)(2,1)S(1)} %scale_hidden.3.hidden_ref, bf16[128,1792]{1,0:T(8,128)(2,1)S(1)} %copy-done.1, bf16[128,1792]{1,0:T(8,128)(2,1)S(1)} %copy-done.15, bf16[128,1792]{1,0:T(8,128)(2,1)S(1)} %copy-done.13, bf16[128,1792]{1,0:T(8,128)(2,1)S(1)} %copy-done.19, ...), custom_call_target="tpu_custom_call" | custom-call | flops 4697620480 | bytes 15466496 | tf_op jit(solution)/shard_map/block_product/pallas_call | solution.py:120
  165.8 2.3 %collective-permute-done.9.refs_6_ = bf16[128,1792]{1,0:T(8,128)(2,1)} collective-permute-done((bf16[128,1792]{1,0:T(8,128)(2,1)}, bf16[128,1792]{1,0:T(8,128)(2,1)}, u32[]{:S(2)}, u32[]{:S(2)}) %collective-permute-start.9) | collective-permute-done | bytes 458784 | tf_op jit(solution)/shard_map/ppermute | solution.py:26
  168.7 8.4 %block_product.5.refs_8_ = bf16[1280,3584]{1,0:T(8,128)(2,1)} custom-call(bf16[1280,1024]{1,0:T(8,128)(2,1)S(1)} %scale_hidden.3.hidden_ref, bf16[128,1792]{1,0:T(8,128)(2,1)S(1)} %get-tuple-element.12.refs_0_, bf16[128,1792]{1,0:T(8,128)(2,1)S(1)} %copy-done.5, bf16[128,1792]{1,0:T(8,128)(2,1)S(1)} %copy-done.3, ...), custom_call_target="tpu_custom_call", output_to_operand_aliasing={{}: (9, {})} | custom-call | flops 4697620480 | bytes 15466496 | tf_op jit(solution)/shard_map/block_product/pallas_call | solution.py:120
  177.1 5.8 %scale_hidden.2.hidden_ref = bf16[1280,1024]{1,0:T(8,128)(2,1)S(1)} custom-call(s32[8]{0:T(128)S(1)} %stack.35.order_ref, bf16[1024,1280]{1,0:T(8,128)(2,1)} %collective-permute-done.hidden_ref, f32[8,1,128]{2,1,0:T(1,128)S(1)} %get-tuple-element.16.gate_ref), custom_call_target="tpu_custom_call" | custom-call | flops 1310720 | bytes 5242880 | tf_op jit(solution)/shard_map/scale_hidden/pallas_call | solution.py:79
  182.9 10.2 %block_product.6.refs_8_ = bf16[1280,3584]{1,0:T(8,128)(2,1)} custom-call(bf16[1280,1024]{1,0:T(8,128)(2,1)S(1)} %scale_hidden.2.hidden_ref, bf16[128,1792]{1,0:T(8,128)(2,1)} %get-tuple-element.13.refs_0_, bf16[128,1792]{1,0:T(8,128)(2,1)} %collective-permute-done.11.refs_1_, ...), custom_call_target="tpu_custom_call", output_to_operand_aliasing={{}: (9, {})} | custom-call | flops 4697620480 | bytes 15466496 | tf_op jit(solution)/shard_map/block_product/pallas_call | solution.py:120
  193.1 9.8 %block_product.7 = bf16[1280,3584]{1,0:T(8,128)(2,1)} custom-call(bf16[1280,1024]{1,0:T(8,128)(2,1)S(1)} %scale_hidden.2.hidden_ref, bf16[128,1792]{1,0:T(8,128)(2,1)S(1)} %get-tuple-element.14.refs_0_, bf16[128,1792]{1,0:T(8,128)(2,1)S(1)} %collective-permute-done.4.refs_1_, ...), custom_call_target="tpu_custom_call", output_to_operand_aliasing={{}: (9, {})} | custom-call | flops 4697620480 | bytes 15466496 | tf_op jit(solution)/shard_map/block_product/pallas_call | solution.py:120
  (109 shorter events, 11.6 us)
Async XLA Ops:
  1.8 16.4 %collective-permute-start.2 = (bf16[128,1792]{1,0:T(8,128)(2,1)S(1)}, bf16[128,1792]{1,0:T(8,128)(2,1)S(1)}, u32[]{:S(2)}, u32[]{:S(2)}) collective-permute-start(bf16[128,1792]{1,0:T(8,128)(2,1)S(1)} %get-tuple-element.12.refs_0_), channel_id=1, source_target_pairs={{0,2},{1,3},{2,4},{3,5},{4,6},{5,7},{6,0},{7,1},{8,10},{9,11},{10,... | collective-permute-start | bytes 1376264 | tf_op jit(solution)/shard_map/ppermute | solution.py:26
  4.9 23.2 %collective-permute-start.24 = (bf16[128,1792]{1,0:T(8,128)(2,1)S(1)}, bf16[128,1792]{1,0:T(8,128)(2,1)S(1)}, u32[]{:S(2)}, u32[]{:S(2)}) collective-permute-start(bf16[128,1792]{1,0:T(8,128)(2,1)S(1)} %get-tuple-element.11.refs_0_), channel_id=1, source_target_pairs={{0,2},{1,3},{2,4},{3,5},{4,6},{5,7},{6,0},{7,1},{8,10},{9,11},{10,... | collective-permute-start | bytes 1376264 | tf_op jit(solution)/shard_map/ppermute | solution.py:26
  18.3 19.8 %collective-permute-start.3 = (bf16[128,1792]{1,0:T(8,128)(2,1)S(1)}, bf16[128,1792]{1,0:T(8,128)(2,1)}, u32[]{:S(2)}, u32[]{:S(2)}) collective-permute-start(bf16[128,1792]{1,0:T(8,128)(2,1)S(1)} %collective-permute-done.2.refs_2_), channel_id=1, source_target_pairs={{0,2},{1,3},{2,4},{3,5},{4,6},{5,7},{6,0},{7,1},{8,10},{9,11},{10,... | collective-permute-start | bytes 1376264 | tf_op jit(solution)/shard_map/ppermute | solution.py:26
  18.3 21.6 %collective-permute-start.1 = (bf16[128,3584]{1,0:T(8,128)(2,1)S(1)}, bf16[128,3584]{1,0:T(8,128)(2,1)S(1)}, u32[]{:S(2)}, u32[]{:S(2)}) collective-permute-start(bf16[128,3584]{1,0:T(8,128)(2,1)S(1)} %get-tuple-element.10), channel_id=1, source_target_pairs={{0,24},{8,16},{16,8},{24,0},{1,25},{9,17},{17,9},{25,1},{2,26},{10... | collective-permute-start | bytes 2752520 | tf_op jit(solution)/shard_map/ppermute | solution.py:16
  21.0 21.6 %collective-permute-start.23 = (bf16[128,1792]{1,0:T(8,128)(2,1)S(1)}, bf16[128,1792]{1,0:T(8,128)(2,1)S(1)}, u32[]{:S(2)}, u32[]{:S(2)}) collective-permute-start(bf16[128,1792]{1,0:T(8,128)(2,1)S(1)} %get-tuple-element.11.refs_0_), channel_id=1, source_target_pairs={{0,1},{1,0},{2,3},{3,2},{4,5},{5,4},{6,7},{7,6},{8,9},{9,8},{10,11... | collective-permute-start | bytes 1376264 | tf_op jit(solution)/shard_map/ppermute | solution.py:21
  21.0 25.9 %collective-permute-start.18 = (bf16[128,1792]{1,0:T(8,128)(2,1)S(1)}, bf16[128,1792]{1,0:T(8,128)(2,1)S(1)}, u32[]{:S(2)}, u32[]{:S(2)}) collective-permute-start(bf16[128,1792]{1,0:T(8,128)(2,1)S(1)} %get-tuple-element.12.refs_0_), channel_id=1, source_target_pairs={{0,1},{1,0},{2,3},{3,2},{4,5},{5,4},{6,7},{7,6},{8,9},{9,8},{10,11... | collective-permute-start | bytes 1376264 | tf_op jit(solution)/shard_map/ppermute | solution.py:21
  28.1 18.8 %collective-permute-start.26 = (bf16[128,1792]{1,0:T(8,128)(2,1)S(1)}, bf16[128,1792]{1,0:T(8,128)(2,1)S(1)}, u32[]{:S(2)}, u32[]{:S(2)}) collective-permute-start(bf16[128,1792]{1,0:T(8,128)(2,1)S(1)} %collective-permute-done.24.refs_2_), channel_id=1, source_target_pairs={{0,2},{1,3},{2,4},{3,5},{4,6},{5,7},{6,0},{7,1},{8,10},{9,11},{10,... | collective-permute-start | bytes 1376264 | tf_op jit(solution)/shard_map/ppermute | solution.py:26
  39.9 128.2 %collective-permute-start = (bf16[1024,1280]{1,0:T(8,128)(2,1)}, bf16[1024,1280]{1,0:T(8,128)(2,1)}, u32[]{:S(2)}, u32[]{:S(2)}) collective-permute-start(bf16[1024,1280]{1,0:T(8,128)(2,1)} %get-tuple-element.8), channel_id=1, source_target_pairs={{0,24},{8,16},{16,8},{24,0},{1,25},{9,17},{17,9},{25,1},{2,26},{10... | collective-permute-start | bytes 7864328 | tf_op jit(solution)/shard_map/ppermute | solution.py:16
  46.9 15.3 %collective-permute-start.28 = (bf16[128,1792]{1,0:T(8,128)(2,1)S(1)}, bf16[128,1792]{1,0:T(8,128)(2,1)S(1)}, u32[]{:S(2)}, u32[]{:S(2)}) collective-permute-start(bf16[128,1792]{1,0:T(8,128)(2,1)S(1)} %collective-permute-done.26.refs_4_), channel_id=1, source_target_pairs={{0,2},{1,3},{2,4},{3,5},{4,6},{5,7},{6,0},{7,1},{8,10},{9,11},{10,... | collective-permute-start | bytes 1376264 | tf_op jit(solution)/shard_map/ppermute | solution.py:26
  47.0 25.0 %collective-permute-start.21 = (bf16[128,1792]{1,0:T(8,128)(2,1)}, bf16[128,1792]{1,0:T(8,128)(2,1)S(1)}, u32[]{:S(2)}, u32[]{:S(2)}) collective-permute-start(bf16[128,1792]{1,0:T(8,128)(2,1)} %collective-permute-done.3.refs_4_), channel_id=1, source_target_pairs={{0,2},{1,3},{2,4},{3,5},{4,6},{5,7},{6,0},{7,1},{8,10},{9,11},{10,... | collective-permute-start | bytes 1376264 | tf_op jit(solution)/shard_map/ppermute | solution.py:26
  49.9 32.0 %collective-permute-start.12 = (bf16[128,1792]{1,0:T(8,128)(2,1)}, bf16[128,1792]{1,0:T(8,128)(2,1)}, u32[]{:S(2)}, u32[]{:S(2)}) collective-permute-start(bf16[128,1792]{1,0:T(8,128)(2,1)} %get-tuple-element.13.refs_0_), channel_id=1, source_target_pairs={{0,2},{1,3},{2,4},{3,5},{4,6},{5,7},{6,0},{7,1},{8,10},{9,11},{10,... | collective-permute-start | bytes 1376264 | tf_op jit(solution)/shard_map/ppermute | solution.py:26
  62.2 19.8 %collective-permute-start.20 = (bf16[128,1792]{1,0:T(8,128)(2,1)}, bf16[128,1792]{1,0:T(8,128)(2,1)}, u32[]{:S(2)}, u32[]{:S(2)}) collective-permute-start(bf16[128,1792]{1,0:T(8,128)(2,1)} %collective-permute-done.3.refs_4_), channel_id=1, source_target_pairs={{0,1},{1,0},{2,3},{3,2},{4,5},{5,4},{6,7},{7,6},{8,9},{9,8},{10,11... | collective-permute-start | bytes 1376264 | tf_op jit(solution)/shard_map/ppermute | solution.py:21
  63.0 19.1 %collective-permute-start.11 = (bf16[128,1792]{1,0:T(8,128)(2,1)}, bf16[128,1792]{1,0:T(8,128)(2,1)}, u32[]{:S(2)}, u32[]{:S(2)}) collective-permute-start(bf16[128,1792]{1,0:T(8,128)(2,1)} %get-tuple-element.13.refs_0_), channel_id=1, source_target_pairs={{0,1},{1,0},{2,3},{3,2},{4,5},{5,4},{6,7},{7,6},{8,9},{9,8},{10,11... | collective-permute-start | bytes 1376264 | tf_op jit(solution)/shard_map/ppermute | solution.py:21
  72.8 19.0 %collective-permute-start.5 = (bf16[128,1792]{1,0:T(8,128)(2,1)S(1)}, bf16[128,1792]{1,0:T(8,128)(2,1)}, u32[]{:S(2)}, u32[]{:S(2)}) collective-permute-start(bf16[128,1792]{1,0:T(8,128)(2,1)S(1)} %get-tuple-element.14.refs_0_), channel_id=1, source_target_pairs={{0,2},{1,3},{2,4},{3,5},{4,6},{5,7},{6,0},{7,1},{8,10},{9,11},{10,... | collective-permute-start | bytes 1376264 | tf_op jit(solution)/shard_map/ppermute | solution.py:26
  82.0 19.7 %collective-permute-start.14 = (bf16[128,1792]{1,0:T(8,128)(2,1)}, bf16[128,1792]{1,0:T(8,128)(2,1)}, u32[]{:S(2)}, u32[]{:S(2)}) collective-permute-start(bf16[128,1792]{1,0:T(8,128)(2,1)} %collective-permute-done.12.refs_2_), channel_id=1, source_target_pairs={{0,2},{1,3},{2,4},{3,5},{4,6},{5,7},{6,0},{7,1},{8,10},{9,11},{10,... | collective-permute-start | bytes 1376264 | tf_op jit(solution)/shard_map/ppermute | solution.py:26
  82.0 69.2 %collective-permute-start.29 = (bf16[128,1792]{1,0:T(8,128)(2,1)}, bf16[128,1792]{1,0:T(8,128)(2,1)S(1)}, u32[]{:S(2)}, u32[]{:S(2)}) collective-permute-start(bf16[128,1792]{1,0:T(8,128)(2,1)} %copy-done.20), channel_id=1, source_target_pairs={{0,1},{1,0},{2,3},{3,2},{4,5},{5,4},{6,7},{7,6},{8,9},{9,8},{10,11... | collective-permute-start | bytes 1376264 | tf_op jit(solution)/shard_map/ppermute | solution.py:21
  82.1 70.2 %collective-permute-start.22 = (bf16[128,1792]{1,0:T(8,128)(2,1)}, bf16[128,1792]{1,0:T(8,128)(2,1)S(1)}, u32[]{:S(2)}, u32[]{:S(2)}) collective-permute-start(bf16[128,1792]{1,0:T(8,128)(2,1)} %copy-done.8), channel_id=1, source_target_pairs={{0,1},{1,0},{2,3},{3,2},{4,5},{5,4},{6,7},{7,6},{8,9},{9,8},{10,11... | collective-permute-start | bytes 1376264 | tf_op jit(solution)/shard_map/ppermute | solution.py:21
  91.8 61.5 %collective-permute-start.7 = (bf16[128,1792]{1,0:T(8,128)(2,1)}, bf16[128,1792]{1,0:T(8,128)(2,1)}, u32[]{:S(2)}, u32[]{:S(2)}) collective-permute-start(bf16[128,1792]{1,0:T(8,128)(2,1)} %collective-permute-done.5.refs_2_), channel_id=1, source_target_pairs={{0,2},{1,3},{2,4},{3,5},{4,6},{5,7},{6,0},{7,1},{8,10},{9,11},{10,... | collective-permute-start | bytes 1376264 | tf_op jit(solution)/shard_map/ppermute | solution.py:26
  101.6 56.3 %collective-permute-start.16 = (bf16[128,1792]{1,0:T(8,128)(2,1)}, bf16[128,1792]{1,0:T(8,128)(2,1)}, u32[]{:S(2)}, u32[]{:S(2)}) collective-permute-start(bf16[128,1792]{1,0:T(8,128)(2,1)} %collective-permute-done.14.refs_4_), channel_id=1, source_target_pairs={{0,2},{1,3},{2,4},{3,5},{4,6},{5,7},{6,0},{7,1},{8,10},{9,11},{10,... | collective-permute-start | bytes 1376264 | tf_op jit(solution)/shard_map/ppermute | solution.py:26
  157.9 25.0 %collective-permute-start.17 = (bf16[128,1792]{1,0:T(8,128)(2,1)}, bf16[128,1792]{1,0:T(8,128)(2,1)S(1)}, u32[]{:S(2)}, u32[]{:S(2)}) collective-permute-start(bf16[128,1792]{1,0:T(8,128)(2,1)} %collective-permute-done.16.refs_6_), channel_id=1, source_target_pairs={{0,1},{1,0},{2,3},{3,2},{4,5},{5,4},{6,7},{7,6},{8,9},{9,8},{10,11... | collective-permute-start | bytes 1376264 | tf_op jit(solution)/shard_map/ppermute | solution.py:21
  165.3 27.7 %collective-permute-start.4 = (bf16[128,1792]{1,0:T(8,128)(2,1)S(1)}, bf16[128,1792]{1,0:T(8,128)(2,1)S(1)}, u32[]{:S(2)}, u32[]{:S(2)}) collective-permute-start(bf16[128,1792]{1,0:T(8,128)(2,1)S(1)} %get-tuple-element.14.refs_0_), channel_id=1, source_target_pairs={{0,1},{1,0},{2,3},{3,2},{4,5},{5,4},{6,7},{7,6},{8,9},{9,8},{10,11... | collective-permute-start | bytes 1376264 | tf_op jit(solution)/shard_map/ppermute | solution.py:21
  165.8 27.3 %collective-permute-start.6 = (bf16[128,1792]{1,0:T(8,128)(2,1)}, bf16[128,1792]{1,0:T(8,128)(2,1)S(1)}, u32[]{:S(2)}, u32[]{:S(2)}) collective-permute-start(bf16[128,1792]{1,0:T(8,128)(2,1)} %collective-permute-done.5.refs_2_), channel_id=1, source_target_pairs={{0,1},{1,0},{2,3},{3,2},{4,5},{5,4},{6,7},{7,6},{8,9},{9,8},{10,11... | collective-permute-start | bytes 1376264 | tf_op jit(solution)/shard_map/ppermute | solution.py:21
  168.2 24.9 %collective-permute-start.8 = (bf16[128,1792]{1,0:T(8,128)(2,1)}, bf16[128,1792]{1,0:T(8,128)(2,1)S(1)}, u32[]{:S(2)}, u32[]{:S(2)}) collective-permute-start(bf16[128,1792]{1,0:T(8,128)(2,1)} %collective-permute-done.7.refs_4_), channel_id=1, source_target_pairs={{0,1},{1,0},{2,3},{3,2},{4,5},{5,4},{6,7},{7,6},{8,9},{9,8},{10,11... | collective-permute-start | bytes 1376264 | tf_op jit(solution)/shard_map/ppermute | solution.py:21
  168.2 24.9 %collective-permute-start.10 = (bf16[128,1792]{1,0:T(8,128)(2,1)}, bf16[128,1792]{1,0:T(8,128)(2,1)S(1)}, u32[]{:S(2)}, u32[]{:S(2)}) collective-permute-start(bf16[128,1792]{1,0:T(8,128)(2,1)} %collective-permute-done.9.refs_6_), channel_id=1, source_target_pairs={{0,1},{1,0},{2,3},{3,2},{4,5},{5,4},{6,7},{7,6},{8,9},{9,8},{10,11... | collective-permute-start | bytes 1376264 | tf_op jit(solution)/shard_map/ppermute | solution.py:21
  (35 other events, 556.6 us)

commit v2 on v1

v2 whole, which is shorter than its diff:
```python
import functools
import jax
import jax.numpy as jnp
from jax import lax
from jax.experimental import pallas as pl
from jax.experimental.pallas import tpu as pltpu
from jax.sharding import PartitionSpec as P

BF16 = jnp.bfloat16
F32 = jnp.float32
LANES = 128
PARTS = 5
TOKEN = (16, 128)
VMEM_SMALL = 8 << 20
VMEM = 24 << 20
VMEM_PACK = 58 << 20
WITH_C = 2
HOLD_D = True
TOK_A = TOK_B = TOK_C = True
C_AFTER = 1
TM_P = 2
SUM = BF16
VMEM_SCALE = 8 << 20
VMEM_FIRST = 24 << 20
CUT = 0.5


def mirror(shard):
    ranks = lax.axis_size("pipe")
    return lax.ppermute(shard, "pipe", [(i, ranks - 1 - i) for i in range(ranks)])


def core_swap(shard):
    count = lax.axis_size("expert")
    return lax.ppermute(shard, "expert", [(i, i ^ 1) for i in range(count)])


def chip_shift(shard):
    count = lax.axis_size("expert")
    return lax.ppermute(shard, "expert", [(i, (i + 2) % count) for i in range(count)])


def build_outbound(token_rows, route_ids, bucket_ids, experts, capacity):
    tok_count, top_count = route_ids.shape
    flat_ids = route_ids.reshape(-1)
    one_hot = (flat_ids[:, None] == jnp.arange(experts, dtype=jnp.int32)[None, :]).astype(jnp.int32)
    earlier = jnp.cumsum(one_hot, axis=0) - one_hot
    position = jnp.sum(earlier * one_hot, axis=1)
    slot_ids = flat_ids * capacity + position
    weighting = bucket_ids.reshape(-1).astype(F32) / 64.0
    slot_table = (
        slot_ids[:, None] == jnp.arange(experts * capacity, dtype=jnp.int32)[None, :]
    ).astype(F32)
    slot_table = slot_table * weighting[:, None]
    spread = jnp.sum(slot_table.reshape(tok_count, top_count, experts * capacity), axis=1).astype(BF16)
    outbound = lax.dot_general(
        spread, token_rows, (((0,), (0,)), ((), ())), preferred_element_type=F32
    )
    return outbound.astype(BF16).reshape(experts, capacity, token_rows.shape[1])


def slot_product(hidden_rows, inbound):
    flat_in = inbound.reshape(-1, inbound.shape[-1])
    product = lax.dot_general(
        hidden_rows, flat_in, (((0,), (0,)), ((), ())), preferred_element_type=F32
    )
    return product.astype(BF16)


def routed(token_rows, route_ids, bucket_ids, hidden_rows, experts, capacity):
    partials = []
    for index in range(2):
        outbound = build_outbound(
            token_rows[index], route_ids[index], bucket_ids[index], experts, capacity
        )
        arrived = lax.all_to_all(outbound, "expert", split_axis=0, concat_axis=0, tiled=True)
        partials.append(slot_product(hidden_rows[index], arrived))
    return (partials[0].astype(F32) + mirror(partials[1]).astype(F32)).astype(BF16)


def moved(count):
    return pl.CostEstimate(flops=0, bytes_accessed=1024, transcendentals=0)


def pack_kernel(spans, has_gates, rows_ref, *refs):
    outs = refs[len(refs) - len(spans) - 1:-1]
    refs[-1][...] = jnp.zeros_like(refs[-1])
    for (lo, hi), out_ref in zip(spans, outs):
        for start in range(lo, hi, LANES):
            out_ref[start - lo:start - lo + LANES, :] = rows_ref[0, 0, :, start:start + LANES]
        if has_gates:
            out_ref[hi - lo:, :] = refs[0][...]


def pack(grad_rows, direction, spans, gates, *deps):
    tokens, width = grad_rows.shape[2:]
    extra = 0 if gates is None else gates.shape[0]
    shapes = [(hi - lo + extra, LANES) for lo, hi in spans]
    in_specs = [pl.BlockSpec((1, 1, tokens, width), lambda i: (direction, 0, 0, 0))]
    operands = [grad_rows]
    if gates is not None:
        in_specs.append(pl.BlockSpec(gates.shape, lambda i: (0, 0)))
        operands.append(gates)
    return pl.pallas_call(
        functools.partial(pack_kernel, spans, gates is not None),
        grid=(1,),
        in_specs=in_specs + [pl.BlockSpec(memory_space=pl.ANY)] * len(deps),
        out_specs=[pl.BlockSpec(shape, lambda i: (0, 0)) for shape in shapes + [TOKEN]],
        out_shape=[jax.ShapeDtypeStruct(shape, BF16) for shape in shapes + [TOKEN]],
        compiler_params=pltpu.CompilerParams(vmem_limit_bytes=VMEM_PACK),
        cost_estimate=moved(4 * tokens * width),
        name="pack_rows",
    )(*operands, *deps)


def pack_second_kernel(span, order_ref, rows_ref, *refs):
    *hidden_refs, _, out_ref, token_ref = refs
    lo, hi = span
    for start in range(lo, hi, LANES):
        out_ref[start - lo:start - lo + LANES, :] = rows_ref[0, 0, :, start:start + LANES]
    for i, ref in enumerate(hidden_refs):
        base = hi - lo + i * ref.shape[4]
        out_ref[base:base + ref.shape[4], :] = ref[0, 0, 0].T
    token_ref[...] = jnp.zeros_like(token_ref)


def pack_second(order, grad_rows, saved_hidden, span, blocks, dep):
    tokens, width = grad_rows.shape[2:]
    out_rows = saved_hidden.shape[4]
    shape = (span[1] - span[0] + len(blocks) * out_rows, LANES)

    def hidden_spec(i):
        return pl.BlockSpec((1, 1, 1, LANES, out_rows), lambda g, order: (1, 0, 0, order[i], 0))

    return pl.pallas_call(
        functools.partial(pack_second_kernel, span),
        grid_spec=pltpu.PrefetchScalarGridSpec(
            num_scalar_prefetch=1,
            grid=(1,),
            in_specs=[pl.BlockSpec((1, 1, tokens, width), lambda g, order: (1, 0, 0, 0))]
            + [hidden_spec(i) for i in blocks]
            + [pl.BlockSpec(memory_space=pl.ANY)],
            out_specs=[
                pl.BlockSpec(shape, lambda g, order: (0, 0)),
                pl.BlockSpec(TOKEN, lambda g, order: (0, 0)),
            ],
        ),
        out_shape=[jax.ShapeDtypeStruct(shape, BF16), jax.ShapeDtypeStruct(TOKEN, BF16)],
        compiler_params=pltpu.CompilerParams(vmem_limit_bytes=VMEM_PACK),
        cost_estimate=moved(1024),
        name="pack_second",
    )(order, grad_rows, *([saved_hidden] * len(blocks)), dep)


def top_kernel(in_ref, *refs):
    refs[-1][...] = in_ref[...]


def top(value, rows, *deps):
    spec = pl.BlockSpec((rows, LANES), lambda i: (0, 0))
    return pl.pallas_call(
        top_kernel,
        grid=(1,),
        in_specs=[spec] + [pl.BlockSpec(memory_space=pl.ANY)] * len(deps),
        out_specs=spec,
        out_shape=jax.ShapeDtypeStruct((rows, LANES), BF16),
        compiler_params=pltpu.CompilerParams(vmem_limit_bytes=VMEM_SMALL),
        cost_estimate=moved(1024),
        name="top_rows",
    )(value, *deps)


def hold_kernel(*refs):
    pass


def hold(value, *deps):
    return pl.pallas_call(
        hold_kernel,
        in_specs=[pl.BlockSpec(memory_space=pl.ANY)] * (1 + len(deps)),
        out_specs=pl.BlockSpec(memory_space=pl.ANY),
        out_shape=jax.ShapeDtypeStruct(value.shape, value.dtype),
        input_output_aliases={0: 0},
        compiler_params=pltpu.CompilerParams(vmem_limit_bytes=VMEM_SMALL),
        cost_estimate=moved(1024),
        name="hold",
    )(value, *deps)


def turn_kernel(hidden_ref, _, out_ref, token_ref):
    slots = hidden_ref.shape[3]
    for i in range(slots // LANES):
        lanes = slice(i * LANES, (i + 1) * LANES)
        out_ref[:, lanes] = hidden_ref[0, 0, 0, lanes, :].T
    token_ref[...] = jnp.zeros_like(token_ref)


def turned(saved_hidden, dep):
    slots, width = saved_hidden.shape[3:]
    return pl.pallas_call(
        turn_kernel,
        grid=(1,),
        in_specs=[
            pl.BlockSpec((1, 1, 1, slots, width), lambda i: (0, 0, 0, 0, 0)),
            pl.BlockSpec(memory_space=pl.ANY),
        ],
        out_specs=[
            pl.BlockSpec((width, slots), lambda i: (0, 0)),
            pl.BlockSpec(TOKEN, lambda i: (0, 0)),
        ],
        out_shape=[jax.ShapeDtypeStruct((width, slots), BF16), jax.ShapeDtypeStruct(TOKEN, BF16)],
        compiler_params=pltpu.CompilerParams(vmem_limit_bytes=VMEM_PACK),
        cost_estimate=moved(1024),
        name="turn_hidden",
    )(saved_hidden, dep)


def first_scale_kernel(rows_ref, hidden_ref, *refs):
    *packet_refs, out_ref, other_ref = refs
    index = lax.broadcasted_iota(jnp.int32, packet_refs[0].shape, 0)
    for i, ref in enumerate(packet_refs):
        lanes = slice(i * LANES, (i + 1) * LANES)
        gates = ref[...].astype(F32)
        first = jnp.sum(jnp.where(index == rows_ref[0], gates, 0.0), axis=0, keepdims=True)
        second = jnp.sum(jnp.where(index == rows_ref[1], gates, 0.0), axis=0, keepdims=True)
        from_lanes = pl.ds(pl.multiple_of(rows_ref[2 + i] * LANES, LANES), LANES)
        out_ref[:, lanes] = (hidden_ref[:, from_lanes].astype(F32) * first).astype(BF16)
        other_ref[:, lanes] = jnp.broadcast_to(second, (other_ref.shape[0], LANES))


def first_scaled(rows, hidden, packets, extra):
    width, slots = hidden.shape
    tile = width // 2
    last = packets[0].shape[0] // extra - 1
    return pl.pallas_call(
        first_scale_kernel,
        grid_spec=pltpu.PrefetchScalarGridSpec(
            num_scalar_prefetch=1,
            grid=(width // tile,),
            in_specs=[pl.BlockSpec((tile, slots), lambda i, row: (i, 0))]
            + [pl.BlockSpec((extra, LANES), lambda i, row: (last, 0)) for _ in packets],
            out_specs=[
                pl.BlockSpec((tile, slots), lambda i, row: (i, 0)),
                pl.BlockSpec((8, slots), lambda i, row: (0, 0)),
            ],
        ),
        out_shape=[
            jax.ShapeDtypeStruct((width, slots), BF16),
            jax.ShapeDtypeStruct((8, slots), F32),
        ],
        compiler_params=pltpu.CompilerParams(vmem_limit_bytes=VMEM_SCALE),
        cost_estimate=moved(1024),
        name="scale_first",
    )(rows, hidden, *packets)


def second_scale_kernel(gates_ref, *refs):
    for i, ref in enumerate(refs[:-1]):
        lanes = slice(i * LANES, (i + 1) * LANES)
        refs[-1][:, lanes] = (ref[...].astype(F32) * gates_ref[:1, lanes]).astype(BF16)


def second_scaled(gates, packets, out_rows):
    in_specs = [pl.BlockSpec(gates.shape, lambda i: (0, 0))]
    operands = [gates]

    def block_spec(start):
        return pl.BlockSpec((pl.Element(out_rows), pl.Element(LANES)), lambda i: (start, 0))

    for packet, start, count in packets:
        for i in range(count):
            in_specs.append(block_spec(start + i * out_rows))
            operands.append(packet)
    shape = (out_rows, gates.shape[1])
    return pl.pallas_call(
        second_scale_kernel,
        grid=(1,),
        in_specs=in_specs,
        out_specs=pl.BlockSpec(shape, lambda i: (0, 0)),
        out_shape=jax.ShapeDtypeStruct(shape, BF16),
        compiler_params=pltpu.CompilerParams(vmem_limit_bytes=VMEM),
        cost_estimate=moved(1024),
        name="scale_second",
    )(*operands)


def product_kernel(count, add, hidden_ref, *refs):
    tile = refs[0].shape[0]
    rows = jnp.concatenate(
        [
            jnp.concatenate([ref[q:q + LANES, :] for q in range(0, tile, LANES)], axis=1)
            for ref in refs[:count]
        ],
        axis=0,
    )
    product = jnp.dot(hidden_ref[...], rows, preferred_element_type=F32)
    if add:
        product = product + refs[count][...].astype(F32)
    refs[-2][...] = product.astype(refs[-2].dtype)
    refs[-1][...] = jnp.zeros_like(refs[-1])


def block_product(hidden, packets, part, tiles, name, start=0, width=None, add=None, into=None, at=0, size=None, dtype=BF16, vmem=None):
    out_rows = hidden.shape[0]
    size = packets[0].shape[0] if size is None else size
    depth = LANES * len(packets)
    tile_m, tile_n = out_rows // tiles[0], size // tiles[1]

    def out_spec(at):
        return pl.BlockSpec(
            (pl.Element(tile_m), pl.Element(tile_n)),
            lambda j, i: (pl.multiple_of(i * tile_m, 16), pl.multiple_of(at + j * tile_n, LANES)),
        )

    in_specs = [pl.BlockSpec((tile_m, depth), lambda j, i: (i, part))]
    in_specs += [
        pl.BlockSpec(
            (pl.Element(tile_n), pl.Element(LANES)),
            lambda j, i: (pl.multiple_of(start + j * tile_n, 16), 0),
        )
        for _ in packets
    ]
    operands = [hidden, *packets]
    if add is not None:
        in_specs.append(out_spec(0))
        operands.append(add)
    aliases = {}
    if into is not None:
        in_specs.append(pl.BlockSpec(memory_space=pl.ANY))
        aliases = {len(operands): 0}
        operands.append(into)
    return pl.pallas_call(
        functools.partial(product_kernel, len(packets), add is not None),
        grid=(tiles[1], tiles[0]),
        in_specs=in_specs,
        out_specs=[out_spec(at), pl.BlockSpec((8, LANES), lambda j, i: (0, 0))],
        out_shape=[
            jax.ShapeDtypeStruct((out_rows, size if width is None else width), dtype),
            jax.ShapeDtypeStruct((8, LANES), F32),
        ],
        input_output_aliases=aliases,
        compiler_params=pltpu.CompilerParams(vmem_limit_bytes=vmem or VMEM),
        cost_estimate=moved(1024),
        name=name,
    )(*operands)


def gathered(grad_rows, route_ids, bucket_ids, saved_hidden, experts):
    tokens, width = grad_rows.shape[2:]
    steps = experts // 2
    me = lax.axis_index("expert")
    order = jnp.stack(
        [2 * lax.rem(me // 2 + steps - i // 2, steps) + (me % 2 ^ i % 2) for i in range(experts)]
    ).astype(jnp.int32)

    named = route_ids[:, None] == jnp.arange(experts, dtype=jnp.int32)[None, :, None, None]
    gates = (jnp.sum(jnp.where(named, bucket_ids[:, None], 0), axis=3).astype(F32) / 64.0).astype(BF16)
    extra = 2 * experts

    half = width // 2
    cut = round(width * CUT / LANES) * LANES
    span_c, span_d = (0, cut), (cut, width)
    out_rows = saved_hidden.shape[4]

    x, c, d = [None] * steps, [None] * steps, [None] * steps
    x[0], token = pack(grad_rows, 0, [(0, width)], gates.reshape(extra, tokens))
    packet_c, token = pack_second(order, grad_rows, saved_hidden, span_c, range(WITH_C), token)
    packet_d, token = pack_second(order, grad_rows, saved_hidden, span_d, range(WITH_C, experts), token)
    packet_c, packet_d = mirror(packet_c), mirror(packet_d)
    hidden_0, token = turned(saved_hidden, token)
    x[1] = hold(chip_shift(x[0]), token)
    x[2] = chip_shift(x[1])
    c[0] = top(packet_c, span_c[1] - span_c[0], x[C_AFTER])
    c[1] = hold(chip_shift(c[0]), x[2])
    x[3] = chip_shift(x[2])
    c[2] = hold(chip_shift(c[1]), x[3])
    c[3] = chip_shift(c[2])

    def paired(packets):
        return [piece for packet in packets for piece in (packet, core_swap(packet))]

    x = paired(x)
    rows = jnp.concatenate([jnp.stack([me, me + experts]).astype(jnp.int32), order])
    hidden_0, gates_1 = first_scaled(rows, hidden_0, x, extra)
    gates_1 = mirror(gates_1)
    sum_c, token = block_product(
        hidden_0, x, 0, (TM_P, 1), "first_c", 0, size=cut, dtype=SUM, vmem=VMEM_FIRST
    )
    d[0] = top(packet_d, span_d[1] - span_d[0], c[2])
    d[1] = chip_shift(d[0])
    d[1] = hold(d[1], token)
    d[2] = chip_shift(d[1])
    sum_d, token = block_product(
        hidden_0, x, 0, (TM_P, 1), "first_d", cut, size=width - cut, dtype=SUM, vmem=VMEM_FIRST
    )
    d[2] = hold(d[2], token)
    d[3] = chip_shift(d[2])
    hidden_1 = second_scaled(
        gates_1,
        [(packet_c, span_c[1] - span_c[0], WITH_C), (packet_d, span_d[1] - span_d[0], experts - WITH_C)],
        out_rows,
    )
    total, token = block_product(
        hidden_1, paired(c), 0, (2, 2), "second_c", width=width, add=sum_c
    )
    sum_d, token_d = block_product(
        hidden_1, paired(d[:-1]), 0, (2, 1), "second_early_d", add=sum_d, dtype=SUM
    )
    last = hold(d[-1], token, token_d) if HOLD_D else d[-1]
    total, _ = block_product(
        hidden_1, paired([last]), steps - 1, (2, 1), "second_last_d",
        width=width, add=sum_d, into=total, at=cut,
    )
    return total


def on_device(grad_rows, expert_ids, gate_buckets, saved_hidden):
    experts = lax.axis_size("expert")
    capacity = saved_hidden.shape[3] // experts
    tok_count, top_count = expert_ids.shape[2:]
    route_ids, bucket_ids = expert_ids[:, 0], gate_buckets[:, 0]
    if top_count == experts and capacity == tok_count == LANES and experts % 8 == 0:
        result = gathered(grad_rows, route_ids, bucket_ids, saved_hidden, experts)
    else:
        result = routed(
            grad_rows[:, 0], route_ids, bucket_ids, saved_hidden[:, 0, 0], experts, capacity
        )
    return result[None, None]


def solution(mesh):
    return jax.shard_map(
        on_device,
        mesh=mesh,
        in_specs=(
            P(None, "pipe", "expert", None),
            P(None, "pipe", "expert", None),
            P(None, "pipe", "expert", None),
            P(None, "pipe", "expert", None, None),
        ),
        out_specs=P("pipe", "expert", None, None),
        check_vma=False,
    )
```

time: 204 us -> 154 us (0.75)
  blocking collectives: 49.6 us -> 0 us
  starting transfers between devices: 18.3 us -> 10.8 us
  waiting for transfers between devices: 82.1 us -> 87.2 us
  Pallas kernels: 43.9 us -> 48 us
  local copies, waits for them, and re-layouts: 8.54 us -> 6.45 us
    all_gather x1 -> x0, blocking collectives: 49.6 us -> none  [gathered(): all_gates = lax.all_gather(gates, ('pipe', 'expert'), axis=0, tiled=False)]
    ppermute x12 -> x9, starting transfers between devices: 9.32 us -> 3.16 us  [chip_shift(): lax.ppermute(shard, 'expert', [(i, (i + 2) % count) for i in range(count)])]
    pallas_call x6 -> x19, Pallas kernels: 43.9 us -> 48 us  [the longest x5 30.2 us: block_product(): pl.pallas_call(functools.partial(product_kernel, len(packets), add is not...]
    ppermute x16 -> x12, waiting for transfers between devices: 0.04 us -> 3.7 us  [core_swap(): return lax.ppermute(shard, 'expert', [(i, i ^ 1) for i in range(count)])]
    squeeze x3 -> x0, local copies, waits for them, and re-layouts: 3.57 us -> none  [the longest x1 1.84 us: gathered(): scaled_0 = scaled_transposed(order, hidden_rows[0], gates_0)]
    unnamed x58 -> x28, local copies, waits for them, and re-layouts: 4 us -> 5.74 us
    ppermute x12 -> x9, waiting for transfers between devices: 81.9 us -> 83.5 us  [chip_shift(): lax.ppermute(shard, 'expert', [(i, (i + 2) % count) for i in range(count)])]
    ppermute x2 -> x3, starting transfers between devices: 5.43 us -> 4.63 us  [mirror(): lax.ppermute(shard, 'pipe', [(i, ranks - 1 - i) for i in range(ranks)])]
  transfers between devices with their start and end apart: 30 -> 24, of which waited for: 11 -> 10; matrix products, arithmetic and copies ran while one was open for 1% -> 0% of each run, Pallas kernels for 17% -> 28%
where the time goes in v2:
time: 154 us
  waiting for transfers between devices  87.2 us (57%)
  Pallas kernels  48 us (31%)
  starting transfers between devices  10.8 us (7%)
  local copies, waits for them, and re-layouts  6.45 us (4%)
    ppermute x9, waiting for transfers between devices, chip_shift(): lax.ppermute(shard, 'expert', [(i, (i + 2) % count) for i in range(count)])  83.5 us
    pallas_call x5, Pallas kernels, block_product(): pl.pallas_call(functools.partial(product_kernel, len(packets), add is not...  30.2 us
    pallas_call x2, Pallas kernels, pack_second(): pl.pallas_call(functools.partial(pack_second_kernel, span), grid_spec=plt...  7.71 us
    unnamed x28, local copies, waits for them, and re-layouts  5.74 us
    ppermute x3, starting transfers between devices, mirror(): lax.ppermute(shard, 'pipe', [(i, ranks - 1 - i) for i in range(ranks)])  4.63 us
    pallas_call x1, Pallas kernels, turned(): pl.pallas_call(turn_kernel, grid=(1,), in_specs=[pl.BlockSpec((1, 1, 1, s...  4.07 us
    ppermute x12, waiting for transfers between devices, core_swap(): return lax.ppermute(shard, 'expert', [(i, i ^ 1) for i in range(count)])  3.7 us
    ppermute x9, starting transfers between devices, chip_shift(): lax.ppermute(shard, 'expert', [(i, (i + 2) % count) for i in range(count)])  3.16 us
  transfers between devices with their start and end apart: 24, of which 10 were waited for; matrix products, arithmetic and copies ran while one was open for 0% of the time, Pallas kernels for 28%

profile of v2, /device:TPU:0, one launch (start us, length us, event | category | flops | bytes accessed | tf_op | source)
XLA Modules:
  0.0 153.9 jit_solution(16133003249107132191)
XLA Ops:
  1.3 2.3 %pack_rows.1 = (bf16[3600,128]{1,0:T(8,128)(2,1)}, bf16[16,128]{1,0:T(8,128)(2,1)}) custom-call(bf16[2,1,128,3584]{3,2,1,0:T(8,128)(2,1)} %rows_ref.5, bf16[16,128]{1,0:T(8,128)(2,1)} %fusion.refs_0_), custom_call_target="tpu_custom_call" | custom-call | bytes 1024 | tf_op jit(solution)/shard_map/pack_rows/pallas_call | solution.py:104
  3.6 3.0 %collective-permute-start.1 = (bf16[3600,128]{1,0:T(8,128)(2,1)}, bf16[3600,128]{1,0:T(8,128)(2,1)S(1)}, u32[]{:S(2)}, u32[]{:S(2)}) collective-permute-start(bf16[3600,128]{1,0:T(8,128)(2,1)} %get-tuple-element.28.refs_0_), channel_id=1, source_target_pairs={{0,2},{1,3},{2,4},{3,5},{4,6},{5,7},{6,0},{7,1},{8,10},{9,11},{10,... | collective-permute-start | bytes 2764808 | tf_op jit(solution)/shard_map/ppermute | solution.py:40
  7.3 3.3 %pack_second.2 = (bf16[4352,128]{1,0:T(8,128)(2,1)}, bf16[16,128]{1,0:T(8,128)(2,1)}) custom-call(s32[8]{0:T(128)} %stack.43.order_ref, bf16[2,1,128,3584]{3,2,1,0:T(8,128)(2,1)} %rows_ref.5, bf16[2,1,1,1024,1280]{4,3,2,1,0:T(8,128)(2,1)} %hidden_ref.1, bf16[2,1,1,1024,1280]{4,3,2,1,0:T(8,128)(2,1)} %hidden_ref.1, bf16[16,128]{1,0:T(8,128)(2,1)} %get-tuple-element.24.refs_2_), custom_call_target="tpu_custom_call" | custom-call | bytes 1024 | tf_op jit(solution)/shard_map/pack_second/pallas_call | solution.py:135
  10.5 2.4 %collective-permute-start.8 = (bf16[4352,128]{1,0:T(8,128)(2,1)}, bf16[4352,128]{1,0:T(8,128)(2,1)S(1)}, u32[]{:S(2)}, u32[]{:S(2)}) collective-permute-start(bf16[4352,128]{1,0:T(8,128)(2,1)} %get-tuple-element.31), channel_id=1, source_target_pairs={{0,24},{8,16},{16,8},{24,0},{1,25},{9,17},{17,9},{25,1},{2,26},{10... | collective-permute-start | bytes 3342344 | tf_op jit(solution)/shard_map/ppermute | solution.py:30
  13.0 4.4 %pack_second.3 = (bf16[9472,128]{1,0:T(8,128)(2,1)}, bf16[16,128]{1,0:T(8,128)(2,1)}) custom-call(s32[8]{0:T(128)} %stack.43.order_ref, bf16[2,1,128,3584]{3,2,1,0:T(8,128)(2,1)} %rows_ref.5, bf16[2,1,1,1024,1280]{4,3,2,1,0:T(8,128)(2,1)} %hidden_ref.1, bf16[2,1,1,1024,1280]{4,3,2,1,0:T(8,128)(2,1)} %hidden_ref.1, bf16[2,1,1,1024,1280]{4,3,2,1,0:T(8,128)(2,1)} %hidden_ref.1, ...), custom_call_target="tpu_custom_call" | custom-call | bytes 1024 | tf_op jit(solution)/shard_map/pack_second/pallas_call | solution.py:135
  17.9 4.1 %turn_hidden.1 = (bf16[1280,1024]{1,0:T(8,128)(2,1)}, bf16[16,128]{1,0:T(8,128)(2,1)}) custom-call(bf16[2,1,1,1024,1280]{4,3,2,1,0:T(8,128)(2,1)} %hidden_ref.1, bf16[16,128]{1,0:T(8,128)(2,1)} %get-tuple-element.26._), custom_call_target="tpu_custom_call" | custom-call | bytes 1024 | tf_op jit(solution)/shard_map/turn_hidden/pallas_call | solution.py:200
  22.0 7.3 %collective-permute-done.1.refs_0_ = bf16[3600,128]{1,0:T(8,128)(2,1)S(1)} collective-permute-done((bf16[3600,128]{1,0:T(8,128)(2,1)}, bf16[3600,128]{1,0:T(8,128)(2,1)S(1)}, u32[]{:S(2)}, u32[]{:S(2)}) %collective-permute-start.1) | collective-permute-done | bytes 921632 | tf_op jit(solution)/shard_map/ppermute | solution.py:40
  30.0 23.5 %collective-permute-done.3.refs_4_.refs_1_ = bf16[3600,128]{1,0:T(8,128)(2,1)} collective-permute-done((bf16[3600,128]{1,0:T(8,128)(2,1)S(1)}, bf16[3600,128]{1,0:T(8,128)(2,1)}, u32[]{:S(2)}, u32[]{:S(2)}) %collective-permute-start.3) | collective-permute-done | bytes 921632 | tf_op jit(solution)/shard_map/ppermute | solution.py:40
  53.6 32.4 %collective-permute-done.10.refs_0_ = bf16[1792,128]{1,0:T(8,128)(2,1)S(1)} collective-permute-done((bf16[1792,128]{1,0:T(8,128)(2,1)S(1)}, bf16[1792,128]{1,0:T(8,128)(2,1)S(1)}, u32[]{:S(2)}, u32[]{:S(2)}) %collective-permute-start.10) | collective-permute-done | bytes 458784 | tf_op jit(solution)/shard_map/ppermute | solution.py:40
  86.6 11.2 %collective-permute-done.11.refs_0_ = bf16[1792,128]{1,0:T(8,128)(2,1)} collective-permute-done((bf16[1792,128]{1,0:T(8,128)(2,1)S(1)}, bf16[1792,128]{1,0:T(8,128)(2,1)}, u32[]{:S(2)}, u32[]{:S(2)}) %collective-permute-start.11) | collective-permute-done | bytes 458784 | tf_op jit(solution)/shard_map/ppermute | solution.py:40
  99.2 0.9 copy-done.5
  100.7 1.3 collective-permute-done.6.refs_7_
  102.0 1.2 copy-done.3
  103.2 1.2 copy-done.6
  104.3 1.7 %copy-done.8 = bf16[1280,1024]{1,0:T(8,128)(2,1)S(1)} copy-done((bf16[1280,1024]{1,0:T(8,128)(2,1)S(1)}, bf16[1280,1024]{1,0:T(8,128)(2,1)}, u32[]{:S(2)}) %copy-start.8) | copy-done | bytes 2621464
  106.1 2.2 %scale_first.1 = (bf16[1280,1024]{1,0:T(8,128)(2,1)S(1)}, f32[8,1024]{1,0:T(8,128)S(1)}) custom-call(s32[10]{0:T(128)S(1)} %concatenate.4.rows_ref, bf16[1280,1024]{1,0:T(8,128)(2,1)S(1)} %copy-done.8, bf16[3600,128]{1,0:T(8,128)(2,1)S(1)} %copy-done.3, bf16[3600,128]{1,0:T(8,128)(2,1)S(1)} %copy-done.6, bf16[3600,128]{1,0:T(8,128)(2,1)S(1)} %hold.6.refs_2_.refs_0_, ...), custom_call_target="tpu_custom_call" | custom-call | bytes 1024 | tf_op jit(solution)/shard_map/scale_first/pallas_call | solution.py:235
  108.3 6.8 %first_c.1 = (bf16[1280,1792]{1,0:T(8,128)(2,1)S(1)}, f32[8,128]{1,0:T(8,128)S(1)}) custom-call(bf16[1280,1024]{1,0:T(8,128)(2,1)S(1)} %get-tuple-element.33.hidden_ref, bf16[3600,128]{1,0:T(8,128)(2,1)S(1)} %copy-done.4, bf16[3600,128]{1,0:T(8,128)(2,1)S(1)} %copy-done.7, bf16[3600,128]{1,0:T(8,128)(2,1)S(1)} %hold.6.refs_2_.refs_0_, ...), custom_call_target="tpu_custom_call" | custom-call | bytes 1024 | tf_op jit(solution)/shard_map/first_c/pallas_call | solution.py:332
  115.9 8.6 %collective-permute-done.18.refs_6_ = bf16[1792,128]{1,0:T(8,128)(2,1)} collective-permute-done((bf16[1792,128]{1,0:T(8,128)(2,1)}, bf16[1792,128]{1,0:T(8,128)(2,1)}, u32[]{:S(2)}, u32[]{:S(2)}) %collective-permute-start.18) | collective-permute-done | bytes 458784 | tf_op jit(solution)/shard_map/ppermute | solution.py:40
  124.5 1.7 %collective-permute-start.7 = (f32[8,1024]{1,0:T(8,128)S(1)}, f32[8,1024]{1,0:T(8,128)S(1)}, u32[]{:S(2)}, u32[]{:S(2)}) collective-permute-start(f32[8,1024]{1,0:T(8,128)S(1)} %get-tuple-element.30), channel_id=1, source_target_pairs={{0,24},{8,16},{16,8},{24,0},{1,25},{9,17},{17,9},{25,1},{2,26},{10... | collective-permute-start | bytes 98312 | tf_op jit(solution)/shard_map/ppermute | solution.py:30
  126.2 6.7 %first_d.1 = (bf16[1280,1792]{1,0:T(8,128)(2,1)S(1)}, f32[8,128]{1,0:T(8,128)S(1)}) custom-call(bf16[1280,1024]{1,0:T(8,128)(2,1)S(1)} %get-tuple-element.33.hidden_ref, bf16[3600,128]{1,0:T(8,128)(2,1)S(1)} %copy-done.4, bf16[3600,128]{1,0:T(8,128)(2,1)S(1)} %copy-done.7, bf16[3600,128]{1,0:T(8,128)(2,1)S(1)} %hold.6.refs_2_.refs_0_, ...), custom_call_target="tpu_custom_call" | custom-call | bytes 1024 | tf_op jit(solution)/shard_map/first_d/pallas_call | solution.py:332
  135.3 8.5 %second_c.1 = (bf16[1280,3584]{1,0:T(8,128)(2,1)}, f32[8,128]{1,0:T(8,128)S(1)}) custom-call(bf16[1280,1024]{1,0:T(8,128)(2,1)S(1)} %scale_second.1.hidden_ref, bf16[1792,128]{1,0:T(8,128)(2,1)S(1)} %copy-done.10, bf16[1792,128]{1,0:T(8,128)(2,1)S(1)} %collective-permute-done.15.refs_1_, bf16[1792,128]{1,0:T(8,128)(2,1)S(1)} %copy-done.12, ...), custom_call_target="tpu_custom_call" | custom-call | bytes 1024 | tf_op jit(solution)/shard_map/second_c/pallas_call | solution.py:332
  143.8 5.2 %second_early_d.1 = (bf16[1280,1792]{1,0:T(8,128)(2,1)S(1)}, f32[8,128]{1,0:T(8,128)S(1)}) custom-call(bf16[1280,1024]{1,0:T(8,128)(2,1)S(1)} %scale_second.1.hidden_ref, bf16[1792,128]{1,0:T(8,128)(2,1)} %top_rows.3.refs_0_, bf16[1792,128]{1,0:T(8,128)(2,1)S(1)} %collective-permute-done.20.refs_1_, bf16[1792,128]{1,0:T(8,128)(2,1)} %hold.9.refs_2_, ...), custom_call_target="tpu_custom_call" | custom-call | bytes 1024 | tf_op jit(solution)/shard_map/second_early_d/pallas_call | solution.py:332
  149.2 1.7 %collective-permute-done.23.refs_1_ = bf16[1792,128]{1,0:T(8,128)(2,1)S(1)} collective-permute-done((bf16[1792,128]{1,0:T(8,128)(2,1)S(1)}, bf16[1792,128]{1,0:T(8,128)(2,1)S(1)}, u32[]{:S(2)}, u32[]{:S(2)}) %collective-permute-start.23) | collective-permute-done | bytes 458784 | tf_op jit(solution)/shard_map/ppermute | solution.py:35
  150.9 3.0 %second_last_d.1 = (bf16[1280,3584]{1,0:T(8,128)(2,1)}, f32[8,128]{1,0:T(8,128)}) custom-call(bf16[1280,1024]{1,0:T(8,128)(2,1)S(1)} %scale_second.1.hidden_ref, bf16[1792,128]{1,0:T(8,128)(2,1)S(1)} %hold.11.refs_0_, bf16[1792,128]{1,0:T(8,128)(2,1)S(1)} %collective-permute-done.23.refs_1_, ...), custom_call_target="tpu_custom_call", output_to_operand_aliasing={{0}: (4, {})} | custom-call | bytes 1024 | tf_op jit(solution)/shard_map/second_last_d/pallas_call | solution.py:332
  (75 shorter events, 9.1 us)
Async XLA Ops:
  3.6 25.7 %collective-permute-start.1 = (bf16[3600,128]{1,0:T(8,128)(2,1)}, bf16[3600,128]{1,0:T(8,128)(2,1)S(1)}, u32[]{:S(2)}, u32[]{:S(2)}) collective-permute-start(bf16[3600,128]{1,0:T(8,128)(2,1)} %get-tuple-element.28.refs_0_), channel_id=1, source_target_pairs={{0,2},{1,3},{2,4},{3,5},{4,6},{5,7},{6,0},{7,1},{8,10},{9,11},{10,... | collective-permute-start | bytes 2764808 | tf_op jit(solution)/shard_map/ppermute | solution.py:40
  10.5 43.0 %collective-permute-start.8 = (bf16[4352,128]{1,0:T(8,128)(2,1)}, bf16[4352,128]{1,0:T(8,128)(2,1)S(1)}, u32[]{:S(2)}, u32[]{:S(2)}) collective-permute-start(bf16[4352,128]{1,0:T(8,128)(2,1)} %get-tuple-element.31), channel_id=1, source_target_pairs={{0,24},{8,16},{16,8},{24,0},{1,25},{9,17},{17,9},{25,1},{2,26},{10... | collective-permute-start | bytes 3342344 | tf_op jit(solution)/shard_map/ppermute | solution.py:30
  17.4 80.9 %collective-permute-start.9 = (bf16[9472,128]{1,0:T(8,128)(2,1)}, bf16[9472,128]{1,0:T(8,128)(2,1)S(1)}, u32[]{:S(2)}, u32[]{:S(2)}) collective-permute-start(bf16[9472,128]{1,0:T(8,128)(2,1)} %get-tuple-element.32), channel_id=1, source_target_pairs={{0,24},{8,16},{16,8},{24,0},{1,25},{9,17},{17,9},{25,1},{2,26},{10... | collective-permute-start | bytes 7274504 | tf_op jit(solution)/shard_map/ppermute | solution.py:30
  30.0 23.5 %collective-permute-start.3 = (bf16[3600,128]{1,0:T(8,128)(2,1)S(1)}, bf16[3600,128]{1,0:T(8,128)(2,1)}, u32[]{:S(2)}, u32[]{:S(2)}) collective-permute-start(bf16[3600,128]{1,0:T(8,128)(2,1)S(1)} %hold.6.refs_2_.refs_0_), channel_id=1, source_target_pairs={{0,2},{1,3},{2,4},{3,5},{4,6},{5,7},{6,0},{7,1},{8,10},{9,11},{10,... | collective-permute-start | bytes 2764808 | tf_op jit(solution)/shard_map/ppermute | solution.py:40
  53.5 44.3 %collective-permute-start.5 = (bf16[3600,128]{1,0:T(8,128)(2,1)}, bf16[3600,128]{1,0:T(8,128)(2,1)}, u32[]{:S(2)}, u32[]{:S(2)}) collective-permute-start(bf16[3600,128]{1,0:T(8,128)(2,1)} %collective-permute-done.3.refs_4_.refs_1_), channel_id=1, source_target_pairs={{0,2},{1,3},{2,4},{3,5},{4,6},{5,7},{6,0},{7,1},{8,10},{9,11},{10,... | collective-permute-start | bytes 2764808 | tf_op jit(solution)/shard_map/ppermute | solution.py:40
  53.6 32.5 %collective-permute-start.10 = (bf16[1792,128]{1,0:T(8,128)(2,1)S(1)}, bf16[1792,128]{1,0:T(8,128)(2,1)S(1)}, u32[]{:S(2)}, u32[]{:S(2)}) collective-permute-start(bf16[1792,128]{1,0:T(8,128)(2,1)S(1)} %top_rows.2.refs_0_), channel_id=1, source_target_pairs={{0,2},{1,3},{2,4},{3,5},{4,6},{5,7},{6,0},{7,1},{8,10},{9,11},{10,... | collective-permute-start | bytes 1376264 | tf_op jit(solution)/shard_map/ppermute | solution.py:40
  86.1 11.8 %collective-permute-start.11 = (bf16[1792,128]{1,0:T(8,128)(2,1)S(1)}, bf16[1792,128]{1,0:T(8,128)(2,1)}, u32[]{:S(2)}, u32[]{:S(2)}) collective-permute-start(bf16[1792,128]{1,0:T(8,128)(2,1)S(1)} %hold.7.refs_2_), channel_id=1, source_target_pairs={{0,2},{1,3},{2,4},{3,5},{4,6},{5,7},{6,0},{7,1},{8,10},{9,11},{10,... | collective-permute-start | bytes 1376264 | tf_op jit(solution)/shard_map/ppermute | solution.py:40
  86.1 13.1 %collective-permute-start = (bf16[3600,128]{1,0:T(8,128)(2,1)S(1)}, bf16[3600,128]{1,0:T(8,128)(2,1)S(1)}, u32[]{:S(2)}, u32[]{:S(2)}) collective-permute-start(bf16[3600,128]{1,0:T(8,128)(2,1)S(1)} %copy-done.2), channel_id=1, source_target_pairs={{0,1},{1,0},{2,3},{3,2},{4,5},{5,4},{6,7},{7,6},{8,9},{9,8},{10,11... | collective-permute-start | bytes 2764808 | tf_op jit(solution)/shard_map/ppermute | solution.py:35
  86.2 14.0 %collective-permute-start.2 = (bf16[3600,128]{1,0:T(8,128)(2,1)S(1)}, bf16[3600,128]{1,0:T(8,128)(2,1)}, u32[]{:S(2)}, u32[]{:S(2)}) collective-permute-start(bf16[3600,128]{1,0:T(8,128)(2,1)S(1)} %hold.6.refs_2_.refs_0_), channel_id=1, source_target_pairs={{0,1},{1,0},{2,3},{3,2},{4,5},{5,4},{6,7},{7,6},{8,9},{9,8},{10,11... | collective-permute-start | bytes 2764808 | tf_op jit(solution)/shard_map/ppermute | solution.py:35
  97.8 2.8 %collective-permute-start.4 = (bf16[3600,128]{1,0:T(8,128)(2,1)}, bf16[3600,128]{1,0:T(8,128)(2,1)}, u32[]{:S(2)}, u32[]{:S(2)}) collective-permute-start(bf16[3600,128]{1,0:T(8,128)(2,1)} %collective-permute-done.3.refs_4_.refs_1_), channel_id=1, source_target_pairs={{0,1},{1,0},{2,3},{3,2},{4,5},{5,4},{6,7},{7,6},{8,9},{9,8},{10,11... | collective-permute-start | bytes 2764808 | tf_op jit(solution)/shard_map/ppermute | solution.py:35
  97.8 4.1 %collective-permute-start.6 = (bf16[3600,128]{1,0:T(8,128)(2,1)}, bf16[3600,128]{1,0:T(8,128)(2,1)}, u32[]{:S(2)}, u32[]{:S(2)}) collective-permute-start(bf16[3600,128]{1,0:T(8,128)(2,1)} %collective-permute-done.5.refs_6_.refs_1_), channel_id=1, source_target_pairs={{0,1},{1,0},{2,3},{3,2},{4,5},{5,4},{6,7},{7,6},{8,9},{9,8},{10,11... | collective-permute-start | bytes 2764808 | tf_op jit(solution)/shard_map/ppermute | solution.py:35
  99.2 15.9 %collective-permute-start.12 = (bf16[1792,128]{1,0:T(8,128)(2,1)}, bf16[1792,128]{1,0:T(8,128)(2,1)}, u32[]{:S(2)}, u32[]{:S(2)}) collective-permute-start(bf16[1792,128]{1,0:T(8,128)(2,1)} %top_rows.3.refs_0_), channel_id=1, source_target_pairs={{0,2},{1,3},{2,4},{3,5},{4,6},{5,7},{6,0},{7,1},{8,10},{9,11},{10,... | collective-permute-start | bytes 1376264 | tf_op jit(solution)/shard_map/ppermute | solution.py:40
  100.1 24.4 %collective-permute-start.18 = (bf16[1792,128]{1,0:T(8,128)(2,1)}, bf16[1792,128]{1,0:T(8,128)(2,1)}, u32[]{:S(2)}, u32[]{:S(2)}) collective-permute-start(bf16[1792,128]{1,0:T(8,128)(2,1)} %hold.8.refs_0_.refs_4_), channel_id=1, source_target_pairs={{0,2},{1,3},{2,4},{3,5},{4,6},{5,7},{6,0},{7,1},{8,10},{9,11},{10,... | collective-permute-start | bytes 1376264 | tf_op jit(solution)/shard_map/ppermute | solution.py:40
  115.1 18.2 %collective-permute-start.13 = (bf16[1792,128]{1,0:T(8,128)(2,1)}, bf16[1792,128]{1,0:T(8,128)(2,1)S(1)}, u32[]{:S(2)}, u32[]{:S(2)}) collective-permute-start(bf16[1792,128]{1,0:T(8,128)(2,1)} %hold.9.refs_2_), channel_id=1, source_target_pairs={{0,2},{1,3},{2,4},{3,5},{4,6},{5,7},{6,0},{7,1},{8,10},{9,11},{10,... | collective-permute-start | bytes 1376264 | tf_op jit(solution)/shard_map/ppermute | solution.py:40
  115.2 18.1 %collective-permute-start.15 = (bf16[1792,128]{1,0:T(8,128)(2,1)S(1)}, bf16[1792,128]{1,0:T(8,128)(2,1)S(1)}, u32[]{:S(2)}, u32[]{:S(2)}) collective-permute-start(bf16[1792,128]{1,0:T(8,128)(2,1)S(1)} %copy-done.10), channel_id=1, source_target_pairs={{0,1},{1,0},{2,3},{3,2},{4,5},{5,4},{6,7},{7,6},{8,9},{9,8},{10,11... | collective-permute-start | bytes 1376264 | tf_op jit(solution)/shard_map/ppermute | solution.py:35
  115.4 18.4 %collective-permute-start.16 = (bf16[1792,128]{1,0:T(8,128)(2,1)S(1)}, bf16[1792,128]{1,0:T(8,128)(2,1)S(1)}, u32[]{:S(2)}, u32[]{:S(2)}) collective-permute-start(bf16[1792,128]{1,0:T(8,128)(2,1)S(1)} %copy-done.12), channel_id=1, source_target_pairs={{0,1},{1,0},{2,3},{3,2},{4,5},{5,4},{6,7},{7,6},{8,9},{9,8},{10,11... | collective-permute-start | bytes 1376264 | tf_op jit(solution)/shard_map/ppermute | solution.py:35
  115.8 18.1 %collective-permute-start.17 = (bf16[1792,128]{1,0:T(8,128)(2,1)}, bf16[1792,128]{1,0:T(8,128)(2,1)S(1)}, u32[]{:S(2)}, u32[]{:S(2)}) collective-permute-start(bf16[1792,128]{1,0:T(8,128)(2,1)} %hold.8.refs_0_.refs_4_), channel_id=1, source_target_pairs={{0,1},{1,0},{2,3},{3,2},{4,5},{5,4},{6,7},{7,6},{8,9},{9,8},{10,11... | collective-permute-start | bytes 1376264 | tf_op jit(solution)/shard_map/ppermute | solution.py:35
  124.5 9.8 %collective-permute-start.7 = (f32[8,1024]{1,0:T(8,128)S(1)}, f32[8,1024]{1,0:T(8,128)S(1)}, u32[]{:S(2)}, u32[]{:S(2)}) collective-permute-start(f32[8,1024]{1,0:T(8,128)S(1)} %get-tuple-element.30), channel_id=1, source_target_pairs={{0,24},{8,16},{16,8},{24,0},{1,25},{9,17},{17,9},{25,1},{2,26},{10... | collective-permute-start | bytes 98312 | tf_op jit(solution)/shard_map/ppermute | solution.py:30
  133.3 2.0 %collective-permute-start.19 = (bf16[1792,128]{1,0:T(8,128)(2,1)}, bf16[1792,128]{1,0:T(8,128)(2,1)S(1)}, u32[]{:S(2)}, u32[]{:S(2)}) collective-permute-start(bf16[1792,128]{1,0:T(8,128)(2,1)} %collective-permute-done.18.refs_6_), channel_id=1, source_target_pairs={{0,1},{1,0},{2,3},{3,2},{4,5},{5,4},{6,7},{7,6},{8,9},{9,8},{10,11... | collective-permute-start | bytes 1376264 | tf_op jit(solution)/shard_map/ppermute | solution.py:35
  133.3 10.5 %collective-permute-start.20 = (bf16[1792,128]{1,0:T(8,128)(2,1)}, bf16[1792,128]{1,0:T(8,128)(2,1)S(1)}, u32[]{:S(2)}, u32[]{:S(2)}) collective-permute-start(bf16[1792,128]{1,0:T(8,128)(2,1)} %top_rows.3.refs_0_), channel_id=1, source_target_pairs={{0,1},{1,0},{2,3},{3,2},{4,5},{5,4},{6,7},{7,6},{8,9},{9,8},{10,11... | collective-permute-start | bytes 1376264 | tf_op jit(solution)/shard_map/ppermute | solution.py:35
  133.8 10.0 %collective-permute-start.21 = (bf16[1792,128]{1,0:T(8,128)(2,1)}, bf16[1792,128]{1,0:T(8,128)(2,1)S(1)}, u32[]{:S(2)}, u32[]{:S(2)}) collective-permute-start(bf16[1792,128]{1,0:T(8,128)(2,1)} %hold.9.refs_2_), channel_id=1, source_target_pairs={{0,1},{1,0},{2,3},{3,2},{4,5},{5,4},{6,7},{7,6},{8,9},{9,8},{10,11... | collective-permute-start | bytes 1376264 | tf_op jit(solution)/shard_map/ppermute | solution.py:35
  133.9 9.9 %collective-permute-start.22 = (bf16[1792,128]{1,0:T(8,128)(2,1)S(1)}, bf16[1792,128]{1,0:T(8,128)(2,1)S(1)}, u32[]{:S(2)}, u32[]{:S(2)}) collective-permute-start(bf16[1792,128]{1,0:T(8,128)(2,1)S(1)} %hold.10.refs_4_), channel_id=1, source_target_pairs={{0,1},{1,0},{2,3},{3,2},{4,5},{5,4},{6,7},{7,6},{8,9},{9,8},{10,11... | collective-permute-start | bytes 1376264 | tf_op jit(solution)/shard_map/ppermute | solution.py:35
  134.3 14.7 %collective-permute-start.14 = (bf16[1792,128]{1,0:T(8,128)(2,1)S(1)}, bf16[1792,128]{1,0:T(8,128)(2,1)S(1)}, u32[]{:S(2)}, u32[]{:S(2)}) collective-permute-start(bf16[1792,128]{1,0:T(8,128)(2,1)S(1)} %hold.10.refs_4_), channel_id=1, source_target_pairs={{0,2},{1,3},{2,4},{3,5},{4,6},{5,7},{6,0},{7,1},{8,10},{9,11},{10,... | collective-permute-start | bytes 1376264 | tf_op jit(solution)/shard_map/ppermute | solution.py:40
  149.0 1.9 %collective-permute-start.23 = (bf16[1792,128]{1,0:T(8,128)(2,1)S(1)}, bf16[1792,128]{1,0:T(8,128)(2,1)S(1)}, u32[]{:S(2)}, u32[]{:S(2)}) collective-permute-start(bf16[1792,128]{1,0:T(8,128)(2,1)S(1)} %hold.11.refs_0_), channel_id=1, source_target_pairs={{0,1},{1,0},{2,3},{3,2},{4,5},{5,4},{6,7},{7,6},{8,9},{9,8},{10,11... | collective-permute-start | bytes 1376264 | tf_op jit(solution)/shard_map/ppermute | solution.py:35
  (14 other events, 192.7 us)

commit v3 on v2

--- a/solution.py
+++ b/solution.py
@@ -14,15 +14,13 @@
 VMEM_SMALL = 8 << 20
 VMEM = 24 << 20
 VMEM_PACK = 58 << 20
-WITH_C = 2
-HOLD_D = True
-TOK_A = TOK_B = TOK_C = True
-C_AFTER = 1
+PINS = {'x1': ['turn'], 'md': ['c0'], 'x2': ['c1'], 'x3': ['c2', 'fc', 'fd'], 'c2': ['x2'], 'c3': ['d1'], 'd0': ['c2'], 'd1': ['lc', 'ld'], 'd3': ['sc', 'ed']}
+ORDER = ['x1', 'c1', 'x2', 'c2', 'md', 'd0', 'scale_0', 'first_c', 'first_d', 'x3', 'scale_late', 'late_c', 'late_d', 'd1', 'c3', 'd2', 'scale_1', 'second_c', 'early_d', 'd3']
+COSTS = {'x1': 20000000000}
 TM_P = 2
-SUM = BF16
 VMEM_SCALE = 8 << 20
 VMEM_FIRST = 24 << 20
-CUT = 0.5
+CUT = 0.5715
 
 
 def mirror(shard):
@@ -82,35 +80,40 @@
     return pl.CostEstimate(flops=0, bytes_accessed=1024, transcendentals=0)
 
 
-def pack_kernel(spans, has_gates, rows_ref, *refs):
-    outs = refs[len(refs) - len(spans) - 1:-1]
-    refs[-1][...] = jnp.zeros_like(refs[-1])
-    for (lo, hi), out_ref in zip(spans, outs):
-        for start in range(lo, hi, LANES):
-            out_ref[start - lo:start - lo + LANES, :] = rows_ref[0, 0, :, start:start + LANES]
-        if has_gates:
-            out_ref[hi - lo:, :] = refs[0][...]
-
-
-def pack(grad_rows, direction, spans, gates, *deps):
+def pack_kernel(cut, rows_ref, ids_ref, gates_ref, x_ref, c_ref, token_ref):
+    width = rows_ref.shape[3]
+    experts = ids_ref.shape[1]
+    for start in range(0, width, LANES):
+        x_ref[start:start + LANES, :] = rows_ref[0, 0, :, start:start + LANES]
+    for start in range(0, cut, LANES):
+        c_ref[start:start + LANES, :] = rows_ref[1, 0, :, start:start + LANES]
+    named = []
+    for direction in range(2):
+        ids, gates = ids_ref[direction], gates_ref[direction]
+        for expert in range(experts):
+            named.append(jnp.sum(jnp.where(ids == expert, gates, 0), axis=0, keepdims=True))
+    named = jnp.concatenate(named, axis=0).astype(F32) / 64.0
+    x_ref[width:, :] = named.astype(BF16)
+    token_ref[...] = jnp.zeros_like(token_ref)
+
+
+def pack(grad_rows, ids, gates, cut):
     tokens, width = grad_rows.shape[2:]
-    extra = 0 if gates is None else gates.shape[0]
-    shapes = [(hi - lo + extra, LANES) for lo, hi in spans]
-    in_specs = [pl.BlockSpec((1, 1, tokens, width), lambda i: (direction, 0, 0, 0))]
-    operands = [grad_rows]
-    if gates is not None:
-        in_specs.append(pl.BlockSpec(gates.shape, lambda i: (0, 0)))
-        operands.append(gates)
-    return pl.pallas_call(
-        functools.partial(pack_kernel, spans, gates is not None),
+    shapes = [(width + 2 * ids.shape[1], LANES), (cut, LANES), TOKEN]
+    return pl.pallas_call(
+        functools.partial(pack_kernel, cut),
         grid=(1,),
-        in_specs=in_specs + [pl.BlockSpec(memory_space=pl.ANY)] * len(deps),
-        out_specs=[pl.BlockSpec(shape, lambda i: (0, 0)) for shape in shapes + [TOKEN]],
-        out_shape=[jax.ShapeDtypeStruct(shape, BF16) for shape in shapes + [TOKEN]],
+        in_specs=[
+            pl.BlockSpec(grad_rows.shape, lambda i: (0, 0, 0, 0)),
+            pl.BlockSpec(ids.shape, lambda i: (0, 0, 0)),
+            pl.BlockSpec(ids.shape, lambda i: (0, 0, 0)),
+        ],
+        out_specs=[pl.BlockSpec(shape, lambda i: (0, 0)) for shape in shapes],
+        out_shape=[jax.ShapeDtypeStruct(shape, BF16) for shape in shapes],
         compiler_params=pltpu.CompilerParams(vmem_limit_bytes=VMEM_PACK),
-        cost_estimate=moved(4 * tokens * width),
-        name="pack_rows",
-    )(*operands, *deps)
+        cost_estimate=moved(1024),
+        name="pack_first",
+    )(grad_rows, ids, gates)
 
 
 def pack_second_kernel(span, order_ref, rows_ref, *refs):
@@ -174,7 +177,7 @@
     pass
 
 
-def hold(value, *deps):
+def hold(value, *deps, flops=0):
     return pl.pallas_call(
         hold_kernel,
         in_specs=[pl.BlockSpec(memory_space=pl.ANY)] * (1 + len(deps)),
@@ -182,7 +185,7 @@
         out_shape=jax.ShapeDtypeStruct(value.shape, value.dtype),
         input_output_aliases={0: 0},
         compiler_params=pltpu.CompilerParams(vmem_limit_bytes=VMEM_SMALL),
-        cost_estimate=moved(1024),
+        cost_estimate=pl.CostEstimate(flops=flops, bytes_accessed=1024, transcendentals=0),
         name="hold",
     )(value, *deps)
 
@@ -230,6 +233,7 @@
 
 def first_scaled(rows, hidden, packets, extra):
     width, slots = hidden.shape
+    depth = LANES * len(packets)
     tile = width // 2
     last = packets[0].shape[0] // extra - 1
     return pl.pallas_call(
@@ -240,13 +244,13 @@
             in_specs=[pl.BlockSpec((tile, slots), lambda i, row: (i, 0))]
             + [pl.BlockSpec((extra, LANES), lambda i, row: (last, 0)) for _ in packets],
             out_specs=[
-                pl.BlockSpec((tile, slots), lambda i, row: (i, 0)),
-                pl.BlockSpec((8, slots), lambda i, row: (0, 0)),
+                pl.BlockSpec((tile, depth), lambda i, row: (i, 0)),
+                pl.BlockSpec((8, depth), lambda i, row: (0, 0)),
             ],
         ),
         out_shape=[
-            jax.ShapeDtypeStruct((width, slots), BF16),
-            jax.ShapeDtypeStruct((8, slots), F32),
+            jax.ShapeDtypeStruct((width, depth), BF16),
+            jax.ShapeDtypeStruct((8, depth), F32),
         ],
         compiler_params=pltpu.CompilerParams(vmem_limit_bytes=VMEM_SCALE),
         cost_estimate=moved(1024),
@@ -254,34 +258,43 @@
     )(rows, hidden, *packets)
 
 
-def second_scale_kernel(gates_ref, *refs):
-    for i, ref in enumerate(refs[:-1]):
+def second_scale_kernel(early_ref, late_ref, *refs):
+    early = early_ref.shape[1]
+    out_ref, token_ref = refs[-2:]
+    token_ref[...] = jnp.zeros_like(token_ref)
+    for i, ref in enumerate(refs[:-2]):
         lanes = slice(i * LANES, (i + 1) * LANES)
-        refs[-1][:, lanes] = (ref[...].astype(F32) * gates_ref[:1, lanes]).astype(BF16)
-
-
-def second_scaled(gates, packets, out_rows):
-    in_specs = [pl.BlockSpec(gates.shape, lambda i: (0, 0))]
-    operands = [gates]
-
-    def block_spec(start):
-        return pl.BlockSpec((pl.Element(out_rows), pl.Element(LANES)), lambda i: (start, 0))
-
-    for packet, start, count in packets:
-        for i in range(count):
-            in_specs.append(block_spec(start + i * out_rows))
-            operands.append(packet)
-    shape = (out_rows, gates.shape[1])
+        if i * LANES < early:
+            gates = early_ref[:1, lanes]
+        else:
+            gates = late_ref[:1, i * LANES - early:(i + 1) * LANES - early]
+        out_ref[:, lanes] = (ref[...].astype(F32) * gates).astype(BF16)
+
+
+def second_scaled(early, late, packet, start, out_rows):
+    slots = early.shape[1] + late.shape[1]
+
+    def block_spec(row):
+        return pl.BlockSpec((pl.Element(out_rows), pl.Element(LANES)), lambda i: (row, 0))
+
+    blocks = [block_spec(start + i * out_rows) for i in range(slots // LANES)]
     return pl.pallas_call(
         second_scale_kernel,
         grid=(1,),
-        in_specs=in_specs,
-        out_specs=pl.BlockSpec(shape, lambda i: (0, 0)),
-        out_shape=jax.ShapeDtypeStruct(shape, BF16),
+        in_specs=[
+            pl.BlockSpec(early.shape, lambda i: (0, 0)),
+            pl.BlockSpec(late.shape, lambda i: (0, 0)),
+        ]
+        + blocks,
+        out_specs=[
+            pl.BlockSpec((out_rows, slots), lambda i: (0, 0)),
+            pl.BlockSpec(TOKEN, lambda i: (0, 0)),
+        ],
+        out_shape=[jax.ShapeDtypeStruct((out_rows, slots), BF16), jax.ShapeDtypeStruct(TOKEN, BF16)],
         compiler_params=pltpu.CompilerParams(vmem_limit_bytes=VMEM),
         cost_estimate=moved(1024),
         name="scale_second",
-    )(*operands)
+    )(early, late, *([packet] * len(blocks)))
 
 
 def product_kernel(count, add, hidden_ref, *refs):
@@ -353,63 +366,113 @@
         [2 * lax.rem(me // 2 + steps - i // 2, steps) + (me % 2 ^ i % 2) for i in range(experts)]
     ).astype(jnp.int32)
 
-    named = route_ids[:, None] == jnp.arange(experts, dtype=jnp.int32)[None, :, None, None]
-    gates = (jnp.sum(jnp.where(named, bucket_ids[:, None], 0), axis=3).astype(F32) / 64.0).astype(BF16)
     extra = 2 * experts
 
-    half = width // 2
     cut = round(width * CUT / LANES) * LANES
     span_c, span_d = (0, cut), (cut, width)
     out_rows = saved_hidden.shape[4]
 
+    done = {}
+
+    def pinned(name, value):
+        deps = [done[dep] for dep in PINS.get(name, ())]
+        return hold(value, *deps, flops=COSTS.get(name, 0)) if deps else value
+
+    def note(name, value):
+        done[name] = value
+        return value
+
     x, c, d = [None] * steps, [None] * steps, [None] * steps
-    x[0], token = pack(grad_rows, 0, [(0, width)], gates.reshape(extra, tokens))
-    packet_c, token = pack_second(order, grad_rows, saved_hidden, span_c, range(WITH_C), token)
-    packet_d, token = pack_second(order, grad_rows, saved_hidden, span_d, range(WITH_C, experts), token)
-    packet_c, packet_d = mirror(packet_c), mirror(packet_d)
+    ids, buckets = jnp.swapaxes(route_ids, 1, 2), jnp.swapaxes(bucket_ids, 1, 2)
+    x[0], packet_c, token = pack(grad_rows, ids, buckets, cut)
+    packet_d, token = pack_second(order, grad_rows, saved_hidden, span_d, range(experts), token)
+    c[0] = note("c0", mirror(packet_c))
     hidden_0, token = turned(saved_hidden, token)
-    x[1] = hold(chip_shift(x[0]), token)
-    x[2] = chip_shift(x[1])
-    c[0] = top(packet_c, span_c[1] - span_c[0], x[C_AFTER])
-    c[1] = hold(chip_shift(c[0]), x[2])
-    x[3] = chip_shift(x[2])
-    c[2] = hold(chip_shift(c[1]), x[3])
-    c[3] = chip_shift(c[2])
+    note("turn", token)
 
     def paired(packets):
         return [piece for packet in packets for piece in (packet, core_swap(packet))]
 
-    x = paired(x)
-    rows = jnp.concatenate([jnp.stack([me, me + experts]).astype(jnp.int32), order])
-    hidden_0, gates_1 = first_scaled(rows, hidden_0, x, extra)
-    gates_1 = mirror(gates_1)
-    sum_c, token = block_product(
-        hidden_0, x, 0, (TM_P, 1), "first_c", 0, size=cut, dtype=SUM, vmem=VMEM_FIRST
+    results = {}
+
+    def move(name):
+        packets, step = dict(x=x, c=c, d=d)[name[0]], int(name[1])
+        if step:
+            packets[step] = note(name, pinned(name, chip_shift(packets[step - 1])))
+        else:
+            pins = [done[dep] for dep in PINS.get(name, ())]
+            packets[0] = note(name, top(results["md"], width - cut, *pins))
+
+    def mirror_d():
+        results["md"] = mirror(pinned("md", packet_d))
+
+    def scale_0():
+        picked = jnp.concatenate([jnp.stack([me, me + experts]).astype(jnp.int32), order[:early]])
+        results["x"] = paired(x[:-1])
+        results["h0"], gates = first_scaled(picked, hidden_0, results["x"], extra)
+        results["g"] = mirror(gates)
+
+    def first_c():
+        results["c"], token = block_product(
+            results["h0"], results["x"], 0, (TM_P, 1), "first_c", 0, size=cut, vmem=VMEM_FIRST
+        )
+        note("fc", token)
+
+    def first_d():
+        results["d"], token = block_product(
+            results["h0"], results["x"], 0, (TM_P, 1), "first_d", cut, size=width - cut, vmem=VMEM_FIRST
+        )
+        note("fd", token)
+
+    def scale_late():
+        picked = jnp.concatenate([jnp.stack([me, me + experts]).astype(jnp.int32), order[early:]])
+        results["xl"] = paired(x[-1:])
+        results["hl"], gates = first_scaled(picked, hidden_0, results["xl"], extra)
+        results["gl"] = mirror(gates)
+
+    def late_c():
+        results["c"], token = block_product(
+            results["hl"], results["xl"], 0, (2, 1), "late_c", 0, size=cut, add=results["c"]
+        )
+        note("lc", token)
+
+    def late_d():
+        results["d"], token = block_product(
+            results["hl"], results["xl"], 0, (2, 1), "late_d", cut, size=width - cut, add=results["d"]
+        )
+        note("ld", token)
+
+    def scale_1():
+        results["h1"], token = second_scaled(
+            results["g"], results["gl"], results["md"], width - cut, out_rows
+        )
+        note("s1", token)
+
+    def second_c():
+        results["total"], token = block_product(
+            results["h1"], paired(c), 0, (2, 2), "second_c", width=width, add=results["c"]
+        )
+        note("sc", token)
+
+    def early_d():
+        results["d"], token = block_product(
+            results["h1"], paired(d[:-1]), 0, (2, 1), "second_early_d", add=results["d"]
+        )
+        note("ed", token)
+
+    early = 2 * (steps - 1)
+    kernels = dict(
+        md=mirror_d, scale_0=scale_0, first_c=first_c, first_d=first_d, scale_late=scale_late, late_c=late_c,
+        late_d=late_d, scale_1=scale_1, second_c=second_c, early_d=early_d,
     )
-    d[0] = top(packet_d, span_d[1] - span_d[0], c[2])
-    d[1] = chip_shift(d[0])
-    d[1] = hold(d[1], token)
-    d[2] = chip_shift(d[1])
-    sum_d, token = block_product(
-        hidden_0, x, 0, (TM_P, 1), "first_d", cut, size=width - cut, dtype=SUM, vmem=VMEM_FIRST
-    )
-    d[2] = hold(d[2], token)
-    d[3] = chip_shift(d[2])
-    hidden_1 = second_scaled(
-        gates_1,
-        [(packet_c, span_c[1] - span_c[0], WITH_C), (packet_d, span_d[1] - span_d[0], experts - WITH_C)],
-        out_rows,
-    )
-    total, token = block_product(
-        hidden_1, paired(c), 0, (2, 2), "second_c", width=width, add=sum_c
-    )
-    sum_d, token_d = block_product(
-        hidden_1, paired(d[:-1]), 0, (2, 1), "second_early_d", add=sum_d, dtype=SUM
-    )
-    last = hold(d[-1], token, token_d) if HOLD_D else d[-1]
+    for name in ORDER:
+        if name in kernels:
+            kernels[name]()
+        else:
+            move(name)
     total, _ = block_product(
-        hidden_1, paired([last]), steps - 1, (2, 1), "second_last_d",
-        width=width, add=sum_d, into=total, at=cut,
+        results["h1"], paired([d[-1]]), steps - 1, (2, 1), "second_last_d",
+        width=width, add=results["d"], into=results["total"], at=cut,
     )
     return total
 

time: 154 us -> 145 us (0.942)
  waiting for transfers between devices: 87.2 us -> 79.3 us
  starting transfers between devices: 10.8 us -> 14 us
  local copies, waits for them, and re-layouts: 6.45 us -> 4.15 us
    ppermute x9, waiting for transfers between devices: 83.5 us -> 71.8 us  [chip_shift(): lax.ppermute(shard, 'expert', [(i, (i + 2) % count) for i in range(count)])]
    ppermute x3 -> x4, waiting for transfers between devices: 0.01 us -> 3.96 us  [mirror(): lax.ppermute(shard, 'pipe', [(i, ranks - 1 - i) for i in range(ranks)])]
    ppermute x3 -> x4, starting transfers between devices: 4.63 us -> 7.88 us  [mirror(): lax.ppermute(shard, 'pipe', [(i, ranks - 1 - i) for i in range(ranks)])]
    pallas_call x2 -> x1, Pallas kernels: 7.71 us -> 4.98 us  [pack_second(): pl.pallas_call(functools.partial(pack_second_kernel, span), grid_spec=plt...]
    unnamed x28 -> x18, local copies, waits for them, and re-layouts: 5.74 us -> 3.4 us
    ppermute x12, starting transfers between devices: 2.99 us -> 1.35 us  [core_swap(): return lax.ppermute(shard, 'expert', [(i, i ^ 1) for i in range(count)])]
    ppermute x9, starting transfers between devices: 3.16 us -> 4.76 us  [chip_shift(): lax.ppermute(shard, 'expert', [(i, (i + 2) % count) for i in range(count)])]
    pallas_call x1 -> x2, Pallas kernels: 2.17 us -> 3.28 us  [first_scaled(): pl.pallas_call(first_scale_kernel, grid_spec=pltpu.PrefetchScalarGridSpec...]
  transfers between devices with their start and end apart: 24 -> 25, of which waited for: 10 -> 13; matrix products, arithmetic and copies ran while one was open for 0% -> 1% of each run, Pallas kernels for 28% -> 29%
where the time goes in v3:
time: 145 us
  waiting for transfers between devices  79.3 us (55%)
  Pallas kernels  47.2 us (33%)
  starting transfers between devices  14 us (10%)
  local copies, waits for them, and re-layouts  4.15 us (3%)
    ppermute x9, waiting for transfers between devices, chip_shift(): lax.ppermute(shard, 'expert', [(i, (i + 2) % count) for i in range(count)])  71.8 us
    pallas_call x7, Pallas kernels, block_product(): pl.pallas_call(functools.partial(product_kernel, len(packets), add is not...  30.6 us
    ppermute x4, starting transfers between devices, mirror(): lax.ppermute(shard, 'pipe', [(i, ranks - 1 - i) for i in range(ranks)])  7.88 us
    pallas_call x1, Pallas kernels, pack_second(): pl.pallas_call(functools.partial(pack_second_kernel, span), grid_spec=plt...  4.98 us
    ppermute x9, starting transfers between devices, chip_shift(): lax.ppermute(shard, 'expert', [(i, (i + 2) % count) for i in range(count)])  4.76 us
    pallas_call x1, Pallas kernels, turned(): pl.pallas_call(turn_kernel, grid=(1,), in_specs=[pl.BlockSpec((1, 1, 1, s...  4.21 us
    ppermute x4, waiting for transfers between devices, mirror(): lax.ppermute(shard, 'pipe', [(i, ranks - 1 - i) for i in range(ranks)])  3.96 us
    ppermute x12, waiting for transfers between devices, core_swap(): return lax.ppermute(shard, 'expert', [(i, i ^ 1) for i in range(count)])  3.59 us
  transfers between devices with their start and end apart: 25, of which 13 were waited for; matrix products, arithmetic and copies ran while one was open for 1% of the time, Pallas kernels for 29%

profile of v3, /device:TPU:0, one launch (start us, length us, event | category | flops | bytes accessed | tf_op | source)
XLA Modules:
  0.0 145.0 jit_solution(2668820136200012086)
XLA Ops:
  0.0 2.9 %pack_first.1 = (bf16[3600,128]{1,0:T(8,128)(2,1)}, bf16[2048,128]{1,0:T(8,128)(2,1)}, bf16[16,128]{1,0:T(8,128)(2,1)}) custom-call(bf16[2,1,128,3584]{3,2,1,0:T(8,128)(2,1)} %rows_ref.3, s32[2,8,128]{2,1,0:T(8,128)} %bitcast.17, s32[2,8,128]{2,1,0:T(8,128)} %bitcast.18), custom_call_target="tpu_custom_call" | custom-call | bytes 1024 | tf_op jit(solution)/shard_map/pack_first/pallas_call | solution.py:103
  2.9 3.0 %collective-permute-start.1 = (bf16[3600,128]{1,0:T(8,128)(2,1)}, bf16[3600,128]{1,0:T(8,128)(2,1)}, u32[]{:S(2)}, u32[]{:S(2)}) collective-permute-start(bf16[3600,128]{1,0:T(8,128)(2,1)} %get-tuple-element.33.refs_0_), channel_id=1, source_target_pairs={{0,2},{1,3},{2,4},{3,5},{4,6},{5,7},{6,0},{7,1},{8,10},{9,11},{10,... | collective-permute-start | bytes 2764808 | tf_op jit(solution)/shard_map/ppermute | solution.py:38
  5.9 2.4 %collective-permute-start.4 = (bf16[2048,128]{1,0:T(8,128)(2,1)}, bf16[2048,128]{1,0:T(8,128)(2,1)S(1)}, u32[]{:S(2)}, u32[]{:S(2)}) collective-permute-start(bf16[2048,128]{1,0:T(8,128)(2,1)} %get-tuple-element.35), channel_id=1, source_target_pairs={{0,24},{8,16},{16,8},{24,0},{1,25},{9,17},{17,9},{25,1},{2,26},{10... | collective-permute-start | bytes 1572872 | tf_op jit(solution)/shard_map/ppermute | solution.py:28
  9.1 5.0 %pack_second.1 = (bf16[11776,128]{1,0:T(8,128)(2,1)}, bf16[16,128]{1,0:T(8,128)(2,1)}) custom-call(s32[8]{0:T(128)} %stack.45.order_ref, bf16[2,1,128,3584]{3,2,1,0:T(8,128)(2,1)} %rows_ref.3, bf16[2,1,1,1024,1280]{4,3,2,1,0:T(8,128)(2,1)} %hidden_ref.1, bf16[2,1,1,1024,1280]{4,3,2,1,0:T(8,128)(2,1)} %hidden_ref.1, ...), custom_call_target="tpu_custom_call" | custom-call | bytes 1024 | tf_op jit(solution)/shard_map/pack_second/pallas_call | solution.py:138
  14.0 4.2 %turn_hidden.1 = (bf16[1280,1024]{1,0:T(8,128)(2,1)}, bf16[16,128]{1,0:T(8,128)(2,1)}) custom-call(bf16[2,1,1,1024,1280]{4,3,2,1,0:T(8,128)(2,1)} %hidden_ref.1, bf16[16,128]{1,0:T(8,128)(2,1)} %get-tuple-element.31._), custom_call_target="tpu_custom_call" | custom-call | bytes 1024 | tf_op jit(solution)/shard_map/turn_hidden/pallas_call | solution.py:203
  18.2 2.2 %collective-permute-done.4.refs_1_.refs_0_ = bf16[2048,128]{1,0:T(8,128)(2,1)S(1)} collective-permute-done((bf16[2048,128]{1,0:T(8,128)(2,1)}, bf16[2048,128]{1,0:T(8,128)(2,1)S(1)}, u32[]{:S(2)}, u32[]{:S(2)}) %collective-permute-start.4) | collective-permute-done | bytes 524320 | tf_op jit(solution)/shard_map/ppermute | solution.py:28
  22.1 2.4 %collective-permute-start.12 = (bf16[11776,128]{1,0:T(8,128)(2,1)}, bf16[11776,128]{1,0:T(8,128)(2,1)S(1)}, u32[]{:S(2)}, u32[]{:S(2)}) collective-permute-start(bf16[11776,128]{1,0:T(8,128)(2,1)} %copy-done.3), channel_id=1, source_target_pairs={{0,24},{8,16},{16,8},{24,0},{1,25},{9,17},{17,9},{25,1},{2,26},{10... | collective-permute-start | bytes 9043976 | tf_op jit(solution)/shard_map/ppermute | solution.py:28
  26.1 3.4 %collective-permute-done.1.refs_0_ = bf16[3600,128]{1,0:T(8,128)(2,1)} collective-permute-done((bf16[3600,128]{1,0:T(8,128)(2,1)}, bf16[3600,128]{1,0:T(8,128)(2,1)}, u32[]{:S(2)}, u32[]{:S(2)}) %collective-permute-start.1) | collective-permute-done | bytes 921632 | tf_op jit(solution)/shard_map/ppermute | solution.py:38
  29.6 11.6 %collective-permute-done.5.refs_1_.refs_2_ = bf16[2048,128]{1,0:T(8,128)(2,1)S(1)} collective-permute-done((bf16[2048,128]{1,0:T(8,128)(2,1)S(1)}, bf16[2048,128]{1,0:T(8,128)(2,1)S(1)}, u32[]{:S(2)}, u32[]{:S(2)}) %collective-permute-start.5) | collective-permute-done | bytes 524320 | tf_op jit(solution)/shard_map/ppermute | solution.py:38
  41.7 19.3 %collective-permute-done.3.refs_0_ = bf16[3600,128]{1,0:T(8,128)(2,1)} collective-permute-done((bf16[3600,128]{1,0:T(8,128)(2,1)}, bf16[3600,128]{1,0:T(8,128)(2,1)}, u32[]{:S(2)}, u32[]{:S(2)}) %collective-permute-start.3) | collective-permute-done | bytes 921632 | tf_op jit(solution)/shard_map/ppermute | solution.py:38
  61.1 9.8 %collective-permute-done.9.refs_0_ = bf16[2048,128]{1,0:T(8,128)(2,1)S(1)} collective-permute-done((bf16[2048,128]{1,0:T(8,128)(2,1)S(1)}, bf16[2048,128]{1,0:T(8,128)(2,1)S(1)}, u32[]{:S(2)}, u32[]{:S(2)}) %collective-permute-start.9) | collective-permute-done | bytes 524320 | tf_op jit(solution)/shard_map/ppermute | solution.py:38
  74.5 5.0 %first_d.1 = (bf16[1280,1536]{1,0:T(8,128)(2,1)S(1)}, f32[8,128]{1,0:T(8,128)S(1)}) custom-call(bf16[1280,768]{1,0:T(8,128)(2,1)S(1)} %get-tuple-element.37.hidden_ref, bf16[3600,128]{1,0:T(8,128)(2,1)} %get-tuple-element.33.refs_0_, bf16[3600,128]{1,0:T(8,128)(2,1)} %collective-permute-done.refs_1_, bf16[3600,128]{1,0:T(8,128)(2,1)} %hold.8.refs_2_, ...), custom_call_target="tpu_custom_call" | custom-call | bytes 1024 | tf_op jit(solution)/shard_map/first_d/pallas_call | solution.py:345
  79.6 6.3 %first_c.1 = (bf16[1280,2048]{1,0:T(8,128)(2,1)S(1)}, f32[8,128]{1,0:T(8,128)S(1)}) custom-call(bf16[1280,768]{1,0:T(8,128)(2,1)S(1)} %get-tuple-element.37.hidden_ref, bf16[3600,128]{1,0:T(8,128)(2,1)} %get-tuple-element.33.refs_0_, bf16[3600,128]{1,0:T(8,128)(2,1)} %collective-permute-done.refs_1_, bf16[3600,128]{1,0:T(8,128)(2,1)} %hold.8.refs_2_, ...), custom_call_target="tpu_custom_call" | custom-call | bytes 1024 | tf_op jit(solution)/shard_map/first_c/pallas_call | solution.py:345
  85.9 8.1 %collective-permute-done.8.refs_0_ = bf16[3600,128]{1,0:T(8,128)(2,1)} collective-permute-done((bf16[3600,128]{1,0:T(8,128)(2,1)}, bf16[3600,128]{1,0:T(8,128)(2,1)}, u32[]{:S(2)}, u32[]{:S(2)}) %collective-permute-start.8) | collective-permute-done | bytes 921632 | tf_op jit(solution)/shard_map/ppermute | solution.py:38
  94.9 1.8 %collective-permute-done.10.refs_1_ = bf16[3600,128]{1,0:T(8,128)(2,1)S(1)} collective-permute-done((bf16[3600,128]{1,0:T(8,128)(2,1)}, bf16[3600,128]{1,0:T(8,128)(2,1)S(1)}, u32[]{:S(2)}, u32[]{:S(2)}) %collective-permute-start.10) | collective-permute-done | bytes 921632 | tf_op jit(solution)/shard_map/ppermute | solution.py:33
  98.4 2.4 %late_d.1 = (bf16[1280,1536]{1,0:T(8,128)(2,1)S(1)}, f32[8,128]{1,0:T(8,128)S(1)}) custom-call(bf16[1280,256]{1,0:T(8,128)(2,1)S(1)} %get-tuple-element.43.hidden_ref, bf16[3600,128]{1,0:T(8,128)(2,1)} %hold.11.refs_0_, bf16[3600,128]{1,0:T(8,128)(2,1)S(1)} %collective-permute-done.10.refs_1_, bf16[1280,1536]{1,0:T(8,128)(2,1)S(1)} %get-tuple-element.46.refs_2_), custom_call_target="tpu_custom_call" | custom-call | bytes 1024 | tf_op jit(solution)/shard_map/late_d/pallas_call | solution.py:345
  100.8 2.8 %late_c.1 = (bf16[1280,2048]{1,0:T(8,128)(2,1)S(1)}, f32[8,128]{1,0:T(8,128)S(1)}) custom-call(bf16[1280,256]{1,0:T(8,128)(2,1)S(1)} %get-tuple-element.43.hidden_ref, bf16[3600,128]{1,0:T(8,128)(2,1)} %hold.11.refs_0_, bf16[3600,128]{1,0:T(8,128)(2,1)S(1)} %collective-permute-done.10.refs_1_, bf16[1280,2048]{1,0:T(8,128)(2,1)S(1)} %get-tuple-element.44.refs_2_), custom_call_target="tpu_custom_call" | custom-call | bytes 1024 | tf_op jit(solution)/shard_map/late_c/pallas_call | solution.py:345
  103.6 4.2 %collective-permute-done.13.refs_0_ = bf16[1536,128]{1,0:T(8,128)(2,1)S(1)} collective-permute-done((bf16[1536,128]{1,0:T(8,128)(2,1)S(1)}, bf16[1536,128]{1,0:T(8,128)(2,1)S(1)}, u32[]{:S(2)}, u32[]{:S(2)}) %collective-permute-start.13) | collective-permute-done | bytes 393248 | tf_op jit(solution)/shard_map/ppermute | solution.py:38
  107.9 11.2 %collective-permute-done.19.refs_0_ = bf16[2048,128]{1,0:T(8,128)(2,1)S(1)} collective-permute-done((bf16[2048,128]{1,0:T(8,128)(2,1)S(1)}, bf16[2048,128]{1,0:T(8,128)(2,1)S(1)}, u32[]{:S(2)}, u32[]{:S(2)}) %collective-permute-start.19) | collective-permute-done | bytes 524320 | tf_op jit(solution)/shard_map/ppermute | solution.py:38
  119.1 2.8 %collective-permute-start.7 = (f32[8,768]{1,0:T(8,128)S(1)}, f32[8,768]{1,0:T(8,128)S(1)}, u32[]{:S(2)}, u32[]{:S(2)}) collective-permute-start(f32[8,768]{1,0:T(8,128)S(1)} %get-tuple-element.36), channel_id=1, source_target_pairs={{0,24},{8,16},{16,8},{24,0},{1,25},{9,17},{17,9},{25,1},{2,26},{10... | collective-permute-start | bytes 73736 | tf_op jit(solution)/shard_map/ppermute | solution.py:28
  123.9 3.2 %collective-permute-done.14.refs_4_ = bf16[1536,128]{1,0:T(8,128)(2,1)S(1)} collective-permute-done((bf16[1536,128]{1,0:T(8,128)(2,1)S(1)}, bf16[1536,128]{1,0:T(8,128)(2,1)S(1)}, u32[]{:S(2)}, u32[]{:S(2)}) %collective-permute-start.14) | collective-permute-done | bytes 393248 | tf_op jit(solution)/shard_map/ppermute | solution.py:38
  128.4 7.6 %second_c.1 = (bf16[1280,3584]{1,0:T(8,128)(2,1)}, f32[8,128]{1,0:T(8,128)S(1)}) custom-call(bf16[1280,1024]{1,0:T(8,128)(2,1)S(1)} %get-tuple-element.42.hidden_ref, bf16[2048,128]{1,0:T(8,128)(2,1)S(1)} %copy-done.5, bf16[2048,128]{1,0:T(8,128)(2,1)S(1)} %collective-permute-done.16.refs_1_, bf16[2048,128]{1,0:T(8,128)(2,1)S(1)} %copy-done.7, ...), custom_call_target="tpu_custom_call" | custom-call | bytes 1024 | tf_op jit(solution)/shard_map/second_c/pallas_call | solution.py:345
  136.1 3.6 %second_early_d.1 = (bf16[1280,1536]{1,0:T(8,128)(2,1)S(1)}, f32[8,128]{1,0:T(8,128)S(1)}) custom-call(bf16[1280,1024]{1,0:T(8,128)(2,1)S(1)} %get-tuple-element.42.hidden_ref, bf16[1536,128]{1,0:T(8,128)(2,1)S(1)} %top_rows.1.refs_0_, bf16[1536,128]{1,0:T(8,128)(2,1)S(1)} %collective-permute-done.21.refs_1_, bf16[1536,128]{1,0:T(8,128)(2,1)S(1)} %hold.13.refs_1_.refs_2_, ...), custom_call_target="tpu_custom_call" | custom-call | bytes 1024 | tf_op jit(solution)/shard_map/second_early_d/pallas_call | solution.py:345
  142.2 2.8 %second_last_d.1 = (bf16[1280,3584]{1,0:T(8,128)(2,1)}, f32[8,128]{1,0:T(8,128)}) custom-call(bf16[1280,1024]{1,0:T(8,128)(2,1)S(1)} %get-tuple-element.42.hidden_ref, bf16[1536,128]{1,0:T(8,128)(2,1)S(1)} %hold.15.refs_0_, bf16[1536,128]{1,0:T(8,128)(2,1)S(1)} %collective-permute-done.24.refs_1_, ...), custom_call_target="tpu_custom_call", output_to_operand_aliasing={{0}: (4, {})} | custom-call | bytes 1024 | tf_op jit(solution)/shard_map/second_last_d/pallas_call | solution.py:345
  (69 shorter events, 16.4 us)
Async XLA Ops:
  2.9 26.6 %collective-permute-start.1 = (bf16[3600,128]{1,0:T(8,128)(2,1)}, bf16[3600,128]{1,0:T(8,128)(2,1)}, u32[]{:S(2)}, u32[]{:S(2)}) collective-permute-start(bf16[3600,128]{1,0:T(8,128)(2,1)} %get-tuple-element.33.refs_0_), channel_id=1, source_target_pairs={{0,2},{1,3},{2,4},{3,5},{4,6},{5,7},{6,0},{7,1},{8,10},{9,11},{10,... | collective-permute-start | bytes 2764808 | tf_op jit(solution)/shard_map/ppermute | solution.py:38
  5.9 14.5 %collective-permute-start.4 = (bf16[2048,128]{1,0:T(8,128)(2,1)}, bf16[2048,128]{1,0:T(8,128)(2,1)S(1)}, u32[]{:S(2)}, u32[]{:S(2)}) collective-permute-start(bf16[2048,128]{1,0:T(8,128)(2,1)} %get-tuple-element.35), channel_id=1, source_target_pairs={{0,24},{8,16},{16,8},{24,0},{1,25},{9,17},{17,9},{25,1},{2,26},{10... | collective-permute-start | bytes 1572872 | tf_op jit(solution)/shard_map/ppermute | solution.py:28
  22.1 72.0 %collective-permute-start.12 = (bf16[11776,128]{1,0:T(8,128)(2,1)}, bf16[11776,128]{1,0:T(8,128)(2,1)S(1)}, u32[]{:S(2)}, u32[]{:S(2)}) collective-permute-start(bf16[11776,128]{1,0:T(8,128)(2,1)} %copy-done.3), channel_id=1, source_target_pairs={{0,24},{8,16},{16,8},{24,0},{1,25},{9,17},{17,9},{25,1},{2,26},{10... | collective-permute-start | bytes 9043976 | tf_op jit(solution)/shard_map/ppermute | solution.py:28
  24.5 16.7 %collective-permute-start.5 = (bf16[2048,128]{1,0:T(8,128)(2,1)S(1)}, bf16[2048,128]{1,0:T(8,128)(2,1)S(1)}, u32[]{:S(2)}, u32[]{:S(2)}) collective-permute-start(bf16[2048,128]{1,0:T(8,128)(2,1)S(1)} %collective-permute-done.4.refs_1_.refs_0_), channel_id=1, source_target_pairs={{0,2},{1,3},{2,4},{3,5},{4,6},{5,7},{6,0},{7,1},{8,10},{9,11},{10,... | collective-permute-start | bytes 1572872 | tf_op jit(solution)/shard_map/ppermute | solution.py:38
  29.6 31.5 %collective-permute-start.3 = (bf16[3600,128]{1,0:T(8,128)(2,1)}, bf16[3600,128]{1,0:T(8,128)(2,1)}, u32[]{:S(2)}, u32[]{:S(2)}) collective-permute-start(bf16[3600,128]{1,0:T(8,128)(2,1)} %hold.8.refs_2_), channel_id=1, source_target_pairs={{0,2},{1,3},{2,4},{3,5},{4,6},{5,7},{6,0},{7,1},{8,10},{9,11},{10,... | collective-permute-start | bytes 2764808 | tf_op jit(solution)/shard_map/ppermute | solution.py:38
  41.2 29.6 %collective-permute-start.9 = (bf16[2048,128]{1,0:T(8,128)(2,1)S(1)}, bf16[2048,128]{1,0:T(8,128)(2,1)S(1)}, u32[]{:S(2)}, u32[]{:S(2)}) collective-permute-start(bf16[2048,128]{1,0:T(8,128)(2,1)S(1)} %collective-permute-done.5.refs_1_.refs_2_), channel_id=1, source_target_pairs={{0,2},{1,3},{2,4},{3,5},{4,6},{5,7},{6,0},{7,1},{8,10},{9,11},{10,... | collective-permute-start | bytes 1572872 | tf_op jit(solution)/shard_map/ppermute | solution.py:38
  41.2 29.7 %collective-permute-start = (bf16[3600,128]{1,0:T(8,128)(2,1)}, bf16[3600,128]{1,0:T(8,128)(2,1)}, u32[]{:S(2)}, u32[]{:S(2)}) collective-permute-start(bf16[3600,128]{1,0:T(8,128)(2,1)} %get-tuple-element.33.refs_0_), channel_id=1, source_target_pairs={{0,1},{1,0},{2,3},{3,2},{4,5},{5,4},{6,7},{7,6},{8,9},{9,8},{10,11... | collective-permute-start | bytes 2764808 | tf_op jit(solution)/shard_map/ppermute | solution.py:33
  41.2 29.7 %collective-permute-start.2 = (bf16[3600,128]{1,0:T(8,128)(2,1)}, bf16[3600,128]{1,0:T(8,128)(2,1)}, u32[]{:S(2)}, u32[]{:S(2)}) collective-permute-start(bf16[3600,128]{1,0:T(8,128)(2,1)} %hold.8.refs_2_), channel_id=1, source_target_pairs={{0,1},{1,0},{2,3},{3,2},{4,5},{5,4},{6,7},{7,6},{8,9},{9,8},{10,11... | collective-permute-start | bytes 2764808 | tf_op jit(solution)/shard_map/ppermute | solution.py:33
  61.0 9.9 %collective-permute-start.6 = (bf16[3600,128]{1,0:T(8,128)(2,1)}, bf16[3600,128]{1,0:T(8,128)(2,1)}, u32[]{:S(2)}, u32[]{:S(2)}) collective-permute-start(bf16[3600,128]{1,0:T(8,128)(2,1)} %hold.9.refs_4_.refs_1_), channel_id=1, source_target_pairs={{0,1},{1,0},{2,3},{3,2},{4,5},{5,4},{6,7},{7,6},{8,9},{9,8},{10,11... | collective-permute-start | bytes 2764808 | tf_op jit(solution)/shard_map/ppermute | solution.py:33
  70.8 23.2 %collective-permute-start.8 = (bf16[3600,128]{1,0:T(8,128)(2,1)}, bf16[3600,128]{1,0:T(8,128)(2,1)}, u32[]{:S(2)}, u32[]{:S(2)}) collective-permute-start(bf16[3600,128]{1,0:T(8,128)(2,1)} %hold.9.refs_4_.refs_1_), channel_id=1, source_target_pairs={{0,2},{1,3},{2,4},{3,5},{4,6},{5,7},{6,0},{7,1},{8,10},{9,11},{10,... | collective-permute-start | bytes 2764808 | tf_op jit(solution)/shard_map/ppermute | solution.py:38
  94.1 2.7 %collective-permute-start.10 = (bf16[3600,128]{1,0:T(8,128)(2,1)}, bf16[3600,128]{1,0:T(8,128)(2,1)S(1)}, u32[]{:S(2)}, u32[]{:S(2)}) collective-permute-start(bf16[3600,128]{1,0:T(8,128)(2,1)} %hold.11.refs_0_), channel_id=1, source_target_pairs={{0,1},{1,0},{2,3},{3,2},{4,5},{5,4},{6,7},{7,6},{8,9},{9,8},{10,11... | collective-permute-start | bytes 2764808 | tf_op jit(solution)/shard_map/ppermute | solution.py:33
  94.1 13.8 %collective-permute-start.13 = (bf16[1536,128]{1,0:T(8,128)(2,1)S(1)}, bf16[1536,128]{1,0:T(8,128)(2,1)S(1)}, u32[]{:S(2)}, u32[]{:S(2)}) collective-permute-start(bf16[1536,128]{1,0:T(8,128)(2,1)S(1)} %top_rows.1.refs_0_), channel_id=1, source_target_pairs={{0,2},{1,3},{2,4},{3,5},{4,6},{5,7},{6,0},{7,1},{8,10},{9,11},{10,... | collective-permute-start | bytes 1179656 | tf_op jit(solution)/shard_map/ppermute | solution.py:38
  94.2 24.9 %collective-permute-start.19 = (bf16[2048,128]{1,0:T(8,128)(2,1)S(1)}, bf16[2048,128]{1,0:T(8,128)(2,1)S(1)}, u32[]{:S(2)}, u32[]{:S(2)}) collective-permute-start(bf16[2048,128]{1,0:T(8,128)(2,1)S(1)} %hold.10.refs_1_.refs_0_.refs_4_), channel_id=1, source_target_pairs={{0,2},{1,3},{2,4},{3,5},{4,6},{5,7},{6,0},{7,1},{8,10},{9,11},{10,... | collective-permute-start | bytes 1572872 | tf_op jit(solution)/shard_map/ppermute | solution.py:38
  94.2 24.9 %collective-permute-start.16 = (bf16[2048,128]{1,0:T(8,128)(2,1)S(1)}, bf16[2048,128]{1,0:T(8,128)(2,1)S(1)}, u32[]{:S(2)}, u32[]{:S(2)}) collective-permute-start(bf16[2048,128]{1,0:T(8,128)(2,1)S(1)} %copy-done.5), channel_id=1, source_target_pairs={{0,1},{1,0},{2,3},{3,2},{4,5},{5,4},{6,7},{7,6},{8,9},{9,8},{10,11... | collective-permute-start | bytes 1572872 | tf_op jit(solution)/shard_map/ppermute | solution.py:33
  94.8 27.1 %collective-permute-start.17 = (bf16[2048,128]{1,0:T(8,128)(2,1)S(1)}, bf16[2048,128]{1,0:T(8,128)(2,1)S(1)}, u32[]{:S(2)}, u32[]{:S(2)}) collective-permute-start(bf16[2048,128]{1,0:T(8,128)(2,1)S(1)} %copy-done.7), channel_id=1, source_target_pairs={{0,1},{1,0},{2,3},{3,2},{4,5},{5,4},{6,7},{7,6},{8,9},{9,8},{10,11... | collective-permute-start | bytes 1572872 | tf_op jit(solution)/shard_map/ppermute | solution.py:33
  96.8 25.3 %collective-permute-start.18 = (bf16[2048,128]{1,0:T(8,128)(2,1)S(1)}, bf16[2048,128]{1,0:T(8,128)(2,1)S(1)}, u32[]{:S(2)}, u32[]{:S(2)}) collective-permute-start(bf16[2048,128]{1,0:T(8,128)(2,1)S(1)} %hold.10.refs_1_.refs_0_.refs_4_), channel_id=1, source_target_pairs={{0,1},{1,0},{2,3},{3,2},{4,5},{5,4},{6,7},{7,6},{8,9},{9,8},{10,11... | collective-permute-start | bytes 1572872 | tf_op jit(solution)/shard_map/ppermute | solution.py:33
  107.9 19.3 %collective-permute-start.14 = (bf16[1536,128]{1,0:T(8,128)(2,1)S(1)}, bf16[1536,128]{1,0:T(8,128)(2,1)S(1)}, u32[]{:S(2)}, u32[]{:S(2)}) collective-permute-start(bf16[1536,128]{1,0:T(8,128)(2,1)S(1)} %hold.13.refs_1_.refs_2_), channel_id=1, source_target_pairs={{0,2},{1,3},{2,4},{3,5},{4,6},{5,7},{6,0},{7,1},{8,10},{9,11},{10,... | collective-permute-start | bytes 1179656 | tf_op jit(solution)/shard_map/ppermute | solution.py:38
  119.1 9.3 %collective-permute-start.20 = (bf16[2048,128]{1,0:T(8,128)(2,1)S(1)}, bf16[2048,128]{1,0:T(8,128)(2,1)S(1)}, u32[]{:S(2)}, u32[]{:S(2)}) collective-permute-start(bf16[2048,128]{1,0:T(8,128)(2,1)S(1)} %hold.14.refs_6_), channel_id=1, source_target_pairs={{0,1},{1,0},{2,3},{3,2},{4,5},{5,4},{6,7},{7,6},{8,9},{9,8},{10,11... | collective-permute-start | bytes 1572872 | tf_op jit(solution)/shard_map/ppermute | solution.py:33
  119.1 4.8 %collective-permute-start.7 = (f32[8,768]{1,0:T(8,128)S(1)}, f32[8,768]{1,0:T(8,128)S(1)}, u32[]{:S(2)}, u32[]{:S(2)}) collective-permute-start(f32[8,768]{1,0:T(8,128)S(1)} %get-tuple-element.36), channel_id=1, source_target_pairs={{0,24},{8,16},{16,8},{24,0},{1,25},{9,17},{17,9},{25,1},{2,26},{10... | collective-permute-start | bytes 73736 | tf_op jit(solution)/shard_map/ppermute | solution.py:28
  121.9 5.3 %collective-permute-start.11 = (f32[8,256]{1,0:T(8,128)S(1)}, f32[8,256]{1,0:T(8,128)S(1)}, u32[]{:S(2)}, u32[]{:S(2)}) collective-permute-start(f32[8,256]{1,0:T(8,128)S(1)} %get-tuple-element.40), channel_id=1, source_target_pairs={{0,24},{8,16},{16,8},{24,0},{1,25},{9,17},{17,9},{25,1},{2,26},{10... | collective-permute-start | bytes 24584 | tf_op jit(solution)/shard_map/ppermute | solution.py:28
  122.1 14.0 %collective-permute-start.21 = (bf16[1536,128]{1,0:T(8,128)(2,1)S(1)}, bf16[1536,128]{1,0:T(8,128)(2,1)S(1)}, u32[]{:S(2)}, u32[]{:S(2)}) collective-permute-start(bf16[1536,128]{1,0:T(8,128)(2,1)S(1)} %top_rows.1.refs_0_), channel_id=1, source_target_pairs={{0,1},{1,0},{2,3},{3,2},{4,5},{5,4},{6,7},{7,6},{8,9},{9,8},{10,11... | collective-permute-start | bytes 1179656 | tf_op jit(solution)/shard_map/ppermute | solution.py:33
  123.9 12.2 %collective-permute-start.22 = (bf16[1536,128]{1,0:T(8,128)(2,1)S(1)}, bf16[1536,128]{1,0:T(8,128)(2,1)S(1)}, u32[]{:S(2)}, u32[]{:S(2)}) collective-permute-start(bf16[1536,128]{1,0:T(8,128)(2,1)S(1)} %hold.13.refs_1_.refs_2_), channel_id=1, source_target_pairs={{0,1},{1,0},{2,3},{3,2},{4,5},{5,4},{6,7},{7,6},{8,9},{9,8},{10,11... | collective-permute-start | bytes 1179656 | tf_op jit(solution)/shard_map/ppermute | solution.py:33
  127.1 8.9 %collective-permute-start.23 = (bf16[1536,128]{1,0:T(8,128)(2,1)S(1)}, bf16[1536,128]{1,0:T(8,128)(2,1)S(1)}, u32[]{:S(2)}, u32[]{:S(2)}) collective-permute-start(bf16[1536,128]{1,0:T(8,128)(2,1)S(1)} %collective-permute-done.14.refs_4_), channel_id=1, source_target_pairs={{0,1},{1,0},{2,3},{3,2},{4,5},{5,4},{6,7},{7,6},{8,9},{9,8},{10,11... | collective-permute-start | bytes 1179656 | tf_op jit(solution)/shard_map/ppermute | solution.py:33
  127.1 13.3 %collective-permute-start.15 = (bf16[1536,128]{1,0:T(8,128)(2,1)S(1)}, bf16[1536,128]{1,0:T(8,128)(2,1)S(1)}, u32[]{:S(2)}, u32[]{:S(2)}) collective-permute-start(bf16[1536,128]{1,0:T(8,128)(2,1)S(1)} %collective-permute-done.14.refs_4_), channel_id=1, source_target_pairs={{0,2},{1,3},{2,4},{3,5},{4,6},{5,7},{6,0},{7,1},{8,10},{9,11},{10,... | collective-permute-start | bytes 1179656 | tf_op jit(solution)/shard_map/ppermute | solution.py:38
  (10 other events, 89.9 us)

commit v4 on v3

--- a/solution.py
+++ b/solution.py
@@ -9,7 +9,6 @@
 BF16 = jnp.bfloat16
 F32 = jnp.float32
 LANES = 128
-PARTS = 5
 TOKEN = (16, 128)
 VMEM_SMALL = 8 << 20
 VMEM = 24 << 20
@@ -17,7 +16,10 @@
 PINS = {'x1': ['turn'], 'md': ['c0'], 'x2': ['c1'], 'x3': ['c2', 'fc', 'fd'], 'c2': ['x2'], 'c3': ['d1'], 'd0': ['c2'], 'd1': ['lc', 'ld'], 'd3': ['sc', 'ed']}
 ORDER = ['x1', 'c1', 'x2', 'c2', 'md', 'd0', 'scale_0', 'first_c', 'first_d', 'x3', 'scale_late', 'late_c', 'late_d', 'd1', 'c3', 'd2', 'scale_1', 'second_c', 'early_d', 'd3']
 COSTS = {'x1': 20000000000}
-TM_P = 2
+WORK = {}
+TM_P = 5
+TILES_C = (2, 2)
+TILES_L = (2, 1)
 VMEM_SCALE = 8 << 20
 VMEM_FIRST = 24 << 20
 CUT = 0.5715
@@ -353,7 +355,7 @@
         ],
         input_output_aliases=aliases,
         compiler_params=pltpu.CompilerParams(vmem_limit_bytes=vmem or VMEM),
-        cost_estimate=moved(1024),
+        cost_estimate=pl.CostEstimate(flops=WORK.get(name, 0), bytes_accessed=1024, transcendentals=0),
         name=name,
     )(*operands)
 
@@ -450,7 +452,7 @@
 
     def second_c():
         results["total"], token = block_product(
-            results["h1"], paired(c), 0, (2, 2), "second_c", width=width, add=results["c"]
+            results["h1"], paired(c), 0, TILES_C, "second_c", width=width, add=results["c"]
         )
         note("sc", token)
 
@@ -471,7 +473,7 @@
         else:
             move(name)
     total, _ = block_product(
-        results["h1"], paired([d[-1]]), steps - 1, (2, 1), "second_last_d",
+        results["h1"], paired([d[-1]]), steps - 1, TILES_L, "second_last_d",
         width=width, add=results["d"], into=results["total"], at=cut,
     )
     return total

time: 145 us -> 145 us (level)
  no operation moved by 1% of the time
where the time goes in v4:
time: 145 us
  waiting for transfers between devices  78.2 us (54%)
  Pallas kernels  48.4 us (33%)
  starting transfers between devices  14 us (10%)
  local copies, waits for them, and re-layouts  4.15 us (3%)
    ppermute x9, waiting for transfers between devices, chip_shift(): lax.ppermute(shard, 'expert', [(i, (i + 2) % count) for i in range(count)])  70.6 us
    pallas_call x7, Pallas kernels, block_product(): pl.pallas_call(functools.partial(product_kernel, len(packets), add is not...  31.7 us
    ppermute x4, starting transfers between devices, mirror(): lax.ppermute(shard, 'pipe', [(i, ranks - 1 - i) for i in range(ranks)])  7.88 us
    pallas_call x1, Pallas kernels, pack_second(): pl.pallas_call(functools.partial(pack_second_kernel, span), grid_spec=plt...  4.98 us
    ppermute x9, starting transfers between devices, chip_shift(): lax.ppermute(shard, 'expert', [(i, (i + 2) % count) for i in range(count)])  4.76 us
    pallas_call x1, Pallas kernels, turned(): pl.pallas_call(turn_kernel, grid=(1,), in_specs=[pl.BlockSpec((1, 1, 1, s...  4.21 us
    ppermute x4, waiting for transfers between devices, mirror(): lax.ppermute(shard, 'pipe', [(i, ranks - 1 - i) for i in range(ranks)])  3.96 us
    ppermute x12, waiting for transfers between devices, core_swap(): return lax.ppermute(shard, 'expert', [(i, i ^ 1) for i in range(count)])  3.59 us
  transfers between devices with their start and end apart: 25, of which 13 were waited for; matrix products, arithmetic and copies ran while one was open for 1% of the time, Pallas kernels for 29%

profile of v4, /device:TPU:0, one launch (start us, length us, event | category | flops | bytes accessed | tf_op | source)
XLA Modules:
  0.0 145.0 jit_solution(5079905132968769391)
XLA Ops:
  0.0 2.9 %pack_first.1 = (bf16[3600,128]{1,0:T(8,128)(2,1)}, bf16[2048,128]{1,0:T(8,128)(2,1)}, bf16[16,128]{1,0:T(8,128)(2,1)}) custom-call(bf16[2,1,128,3584]{3,2,1,0:T(8,128)(2,1)} %rows_ref.3, s32[2,8,128]{2,1,0:T(8,128)} %bitcast.17, s32[2,8,128]{2,1,0:T(8,128)} %bitcast.18), custom_call_target="tpu_custom_call" | custom-call | bytes 1024 | tf_op jit(solution)/shard_map/pack_first/pallas_call | solution.py:105
  2.9 3.0 %collective-permute-start.1 = (bf16[3600,128]{1,0:T(8,128)(2,1)}, bf16[3600,128]{1,0:T(8,128)(2,1)}, u32[]{:S(2)}, u32[]{:S(2)}) collective-permute-start(bf16[3600,128]{1,0:T(8,128)(2,1)} %get-tuple-element.33.refs_0_), channel_id=1, source_target_pairs={{0,2},{1,3},{2,4},{3,5},{4,6},{5,7},{6,0},{7,1},{8,10},{9,11},{10,... | collective-permute-start | bytes 2764808 | tf_op jit(solution)/shard_map/ppermute | solution.py:40
  5.9 2.4 %collective-permute-start.4 = (bf16[2048,128]{1,0:T(8,128)(2,1)}, bf16[2048,128]{1,0:T(8,128)(2,1)S(1)}, u32[]{:S(2)}, u32[]{:S(2)}) collective-permute-start(bf16[2048,128]{1,0:T(8,128)(2,1)} %get-tuple-element.35), channel_id=1, source_target_pairs={{0,24},{8,16},{16,8},{24,0},{1,25},{9,17},{17,9},{25,1},{2,26},{10... | collective-permute-start | bytes 1572872 | tf_op jit(solution)/shard_map/ppermute | solution.py:30
  9.1 5.0 %pack_second.1 = (bf16[11776,128]{1,0:T(8,128)(2,1)}, bf16[16,128]{1,0:T(8,128)(2,1)}) custom-call(s32[8]{0:T(128)} %stack.45.order_ref, bf16[2,1,128,3584]{3,2,1,0:T(8,128)(2,1)} %rows_ref.3, bf16[2,1,1,1024,1280]{4,3,2,1,0:T(8,128)(2,1)} %hidden_ref.1, bf16[2,1,1,1024,1280]{4,3,2,1,0:T(8,128)(2,1)} %hidden_ref.1, ...), custom_call_target="tpu_custom_call" | custom-call | bytes 1024 | tf_op jit(solution)/shard_map/pack_second/pallas_call | solution.py:140
  14.0 4.2 %turn_hidden.1 = (bf16[1280,1024]{1,0:T(8,128)(2,1)}, bf16[16,128]{1,0:T(8,128)(2,1)}) custom-call(bf16[2,1,1,1024,1280]{4,3,2,1,0:T(8,128)(2,1)} %hidden_ref.1, bf16[16,128]{1,0:T(8,128)(2,1)} %get-tuple-element.31._), custom_call_target="tpu_custom_call" | custom-call | bytes 1024 | tf_op jit(solution)/shard_map/turn_hidden/pallas_call | solution.py:205
  18.2 2.2 %collective-permute-done.4.refs_1_.refs_0_ = bf16[2048,128]{1,0:T(8,128)(2,1)S(1)} collective-permute-done((bf16[2048,128]{1,0:T(8,128)(2,1)}, bf16[2048,128]{1,0:T(8,128)(2,1)S(1)}, u32[]{:S(2)}, u32[]{:S(2)}) %collective-permute-start.4) | collective-permute-done | bytes 524320 | tf_op jit(solution)/shard_map/ppermute | solution.py:30
  22.1 2.4 %collective-permute-start.12 = (bf16[11776,128]{1,0:T(8,128)(2,1)}, bf16[11776,128]{1,0:T(8,128)(2,1)S(1)}, u32[]{:S(2)}, u32[]{:S(2)}) collective-permute-start(bf16[11776,128]{1,0:T(8,128)(2,1)} %copy-done.3), channel_id=1, source_target_pairs={{0,24},{8,16},{16,8},{24,0},{1,25},{9,17},{17,9},{25,1},{2,26},{10... | collective-permute-start | bytes 9043976 | tf_op jit(solution)/shard_map/ppermute | solution.py:30
  26.1 3.4 %collective-permute-done.1.refs_0_ = bf16[3600,128]{1,0:T(8,128)(2,1)} collective-permute-done((bf16[3600,128]{1,0:T(8,128)(2,1)}, bf16[3600,128]{1,0:T(8,128)(2,1)}, u32[]{:S(2)}, u32[]{:S(2)}) %collective-permute-start.1) | collective-permute-done | bytes 921632 | tf_op jit(solution)/shard_map/ppermute | solution.py:40
  29.6 11.6 %collective-permute-done.5.refs_1_.refs_2_ = bf16[2048,128]{1,0:T(8,128)(2,1)S(1)} collective-permute-done((bf16[2048,128]{1,0:T(8,128)(2,1)S(1)}, bf16[2048,128]{1,0:T(8,128)(2,1)S(1)}, u32[]{:S(2)}, u32[]{:S(2)}) %collective-permute-start.5) | collective-permute-done | bytes 524320 | tf_op jit(solution)/shard_map/ppermute | solution.py:40
  41.7 19.3 %collective-permute-done.3.refs_0_ = bf16[3600,128]{1,0:T(8,128)(2,1)} collective-permute-done((bf16[3600,128]{1,0:T(8,128)(2,1)}, bf16[3600,128]{1,0:T(8,128)(2,1)}, u32[]{:S(2)}, u32[]{:S(2)}) %collective-permute-start.3) | collective-permute-done | bytes 921632 | tf_op jit(solution)/shard_map/ppermute | solution.py:40
  61.1 9.8 %collective-permute-done.9.refs_0_ = bf16[2048,128]{1,0:T(8,128)(2,1)S(1)} collective-permute-done((bf16[2048,128]{1,0:T(8,128)(2,1)S(1)}, bf16[2048,128]{1,0:T(8,128)(2,1)S(1)}, u32[]{:S(2)}, u32[]{:S(2)}) %collective-permute-start.9) | collective-permute-done | bytes 524320 | tf_op jit(solution)/shard_map/ppermute | solution.py:40
  74.5 5.6 %first_d.1 = (bf16[1280,1536]{1,0:T(8,128)(2,1)S(1)}, f32[8,128]{1,0:T(8,128)S(1)}) custom-call(bf16[1280,768]{1,0:T(8,128)(2,1)S(1)} %get-tuple-element.37.hidden_ref, bf16[3600,128]{1,0:T(8,128)(2,1)} %get-tuple-element.33.refs_0_, bf16[3600,128]{1,0:T(8,128)(2,1)} %collective-permute-done.refs_1_, bf16[3600,128]{1,0:T(8,128)(2,1)} %hold.8.refs_2_, ...), custom_call_target="tpu_custom_call" | custom-call | bytes 1024 | tf_op jit(solution)/shard_map/first_d/pallas_call | solution.py:347
  80.2 6.9 %first_c.1 = (bf16[1280,2048]{1,0:T(8,128)(2,1)S(1)}, f32[8,128]{1,0:T(8,128)S(1)}) custom-call(bf16[1280,768]{1,0:T(8,128)(2,1)S(1)} %get-tuple-element.37.hidden_ref, bf16[3600,128]{1,0:T(8,128)(2,1)} %get-tuple-element.33.refs_0_, bf16[3600,128]{1,0:T(8,128)(2,1)} %collective-permute-done.refs_1_, bf16[3600,128]{1,0:T(8,128)(2,1)} %hold.8.refs_2_, ...), custom_call_target="tpu_custom_call" | custom-call | bytes 1024 | tf_op jit(solution)/shard_map/first_c/pallas_call | solution.py:347
  87.1 7.0 %collective-permute-done.8.refs_0_ = bf16[3600,128]{1,0:T(8,128)(2,1)} collective-permute-done((bf16[3600,128]{1,0:T(8,128)(2,1)}, bf16[3600,128]{1,0:T(8,128)(2,1)}, u32[]{:S(2)}, u32[]{:S(2)}) %collective-permute-start.8) | collective-permute-done | bytes 921632 | tf_op jit(solution)/shard_map/ppermute | solution.py:40
  94.9 1.8 %collective-permute-done.10.refs_1_ = bf16[3600,128]{1,0:T(8,128)(2,1)S(1)} collective-permute-done((bf16[3600,128]{1,0:T(8,128)(2,1)}, bf16[3600,128]{1,0:T(8,128)(2,1)S(1)}, u32[]{:S(2)}, u32[]{:S(2)}) %collective-permute-start.10) | collective-permute-done | bytes 921632 | tf_op jit(solution)/shard_map/ppermute | solution.py:35
  98.4 2.4 %late_d.1 = (bf16[1280,1536]{1,0:T(8,128)(2,1)S(1)}, f32[8,128]{1,0:T(8,128)S(1)}) custom-call(bf16[1280,256]{1,0:T(8,128)(2,1)S(1)} %get-tuple-element.43.hidden_ref, bf16[3600,128]{1,0:T(8,128)(2,1)} %hold.11.refs_0_, bf16[3600,128]{1,0:T(8,128)(2,1)S(1)} %collective-permute-done.10.refs_1_, bf16[1280,1536]{1,0:T(8,128)(2,1)S(1)} %get-tuple-element.46.refs_2_), custom_call_target="tpu_custom_call" | custom-call | bytes 1024 | tf_op jit(solution)/shard_map/late_d/pallas_call | solution.py:347
  100.8 2.8 %late_c.1 = (bf16[1280,2048]{1,0:T(8,128)(2,1)S(1)}, f32[8,128]{1,0:T(8,128)S(1)}) custom-call(bf16[1280,256]{1,0:T(8,128)(2,1)S(1)} %get-tuple-element.43.hidden_ref, bf16[3600,128]{1,0:T(8,128)(2,1)} %hold.11.refs_0_, bf16[3600,128]{1,0:T(8,128)(2,1)S(1)} %collective-permute-done.10.refs_1_, bf16[1280,2048]{1,0:T(8,128)(2,1)S(1)} %get-tuple-element.44.refs_2_), custom_call_target="tpu_custom_call" | custom-call | bytes 1024 | tf_op jit(solution)/shard_map/late_c/pallas_call | solution.py:347
  103.6 4.2 %collective-permute-done.13.refs_0_ = bf16[1536,128]{1,0:T(8,128)(2,1)S(1)} collective-permute-done((bf16[1536,128]{1,0:T(8,128)(2,1)S(1)}, bf16[1536,128]{1,0:T(8,128)(2,1)S(1)}, u32[]{:S(2)}, u32[]{:S(2)}) %collective-permute-start.13) | collective-permute-done | bytes 393248 | tf_op jit(solution)/shard_map/ppermute | solution.py:40
  107.9 11.2 %collective-permute-done.19.refs_0_ = bf16[2048,128]{1,0:T(8,128)(2,1)S(1)} collective-permute-done((bf16[2048,128]{1,0:T(8,128)(2,1)S(1)}, bf16[2048,128]{1,0:T(8,128)(2,1)S(1)}, u32[]{:S(2)}, u32[]{:S(2)}) %collective-permute-start.19) | collective-permute-done | bytes 524320 | tf_op jit(solution)/shard_map/ppermute | solution.py:40
  119.1 2.8 %collective-permute-start.7 = (f32[8,768]{1,0:T(8,128)S(1)}, f32[8,768]{1,0:T(8,128)S(1)}, u32[]{:S(2)}, u32[]{:S(2)}) collective-permute-start(f32[8,768]{1,0:T(8,128)S(1)} %get-tuple-element.36), channel_id=1, source_target_pairs={{0,24},{8,16},{16,8},{24,0},{1,25},{9,17},{17,9},{25,1},{2,26},{10... | collective-permute-start | bytes 73736 | tf_op jit(solution)/shard_map/ppermute | solution.py:30
  123.9 3.2 %collective-permute-done.14.refs_4_ = bf16[1536,128]{1,0:T(8,128)(2,1)S(1)} collective-permute-done((bf16[1536,128]{1,0:T(8,128)(2,1)S(1)}, bf16[1536,128]{1,0:T(8,128)(2,1)S(1)}, u32[]{:S(2)}, u32[]{:S(2)}) %collective-permute-start.14) | collective-permute-done | bytes 393248 | tf_op jit(solution)/shard_map/ppermute | solution.py:40
  128.4 7.6 %second_c.1 = (bf16[1280,3584]{1,0:T(8,128)(2,1)}, f32[8,128]{1,0:T(8,128)S(1)}) custom-call(bf16[1280,1024]{1,0:T(8,128)(2,1)S(1)} %get-tuple-element.42.hidden_ref, bf16[2048,128]{1,0:T(8,128)(2,1)S(1)} %copy-done.5, bf16[2048,128]{1,0:T(8,128)(2,1)S(1)} %collective-permute-done.16.refs_1_, bf16[2048,128]{1,0:T(8,128)(2,1)S(1)} %copy-done.7, ...), custom_call_target="tpu_custom_call" | custom-call | bytes 1024 | tf_op jit(solution)/shard_map/second_c/pallas_call | solution.py:347
  136.1 3.6 %second_early_d.1 = (bf16[1280,1536]{1,0:T(8,128)(2,1)S(1)}, f32[8,128]{1,0:T(8,128)S(1)}) custom-call(bf16[1280,1024]{1,0:T(8,128)(2,1)S(1)} %get-tuple-element.42.hidden_ref, bf16[1536,128]{1,0:T(8,128)(2,1)S(1)} %top_rows.1.refs_0_, bf16[1536,128]{1,0:T(8,128)(2,1)S(1)} %collective-permute-done.21.refs_1_, bf16[1536,128]{1,0:T(8,128)(2,1)S(1)} %hold.13.refs_1_.refs_2_, ...), custom_call_target="tpu_custom_call" | custom-call | bytes 1024 | tf_op jit(solution)/shard_map/second_early_d/pallas_call | solution.py:347
  142.2 2.8 %second_last_d.1 = (bf16[1280,3584]{1,0:T(8,128)(2,1)}, f32[8,128]{1,0:T(8,128)}) custom-call(bf16[1280,1024]{1,0:T(8,128)(2,1)S(1)} %get-tuple-element.42.hidden_ref, bf16[1536,128]{1,0:T(8,128)(2,1)S(1)} %hold.15.refs_0_, bf16[1536,128]{1,0:T(8,128)(2,1)S(1)} %collective-permute-done.24.refs_1_, ...), custom_call_target="tpu_custom_call", output_to_operand_aliasing={{0}: (4, {})} | custom-call | bytes 1024 | tf_op jit(solution)/shard_map/second_last_d/pallas_call | solution.py:347
  (69 shorter events, 16.4 us)
Async XLA Ops:
  2.9 26.6 %collective-permute-start.1 = (bf16[3600,128]{1,0:T(8,128)(2,1)}, bf16[3600,128]{1,0:T(8,128)(2,1)}, u32[]{:S(2)}, u32[]{:S(2)}) collective-permute-start(bf16[3600,128]{1,0:T(8,128)(2,1)} %get-tuple-element.33.refs_0_), channel_id=1, source_target_pairs={{0,2},{1,3},{2,4},{3,5},{4,6},{5,7},{6,0},{7,1},{8,10},{9,11},{10,... | collective-permute-start | bytes 2764808 | tf_op jit(solution)/shard_map/ppermute | solution.py:40
  5.9 14.5 %collective-permute-start.4 = (bf16[2048,128]{1,0:T(8,128)(2,1)}, bf16[2048,128]{1,0:T(8,128)(2,1)S(1)}, u32[]{:S(2)}, u32[]{:S(2)}) collective-permute-start(bf16[2048,128]{1,0:T(8,128)(2,1)} %get-tuple-element.35), channel_id=1, source_target_pairs={{0,24},{8,16},{16,8},{24,0},{1,25},{9,17},{17,9},{25,1},{2,26},{10... | collective-permute-start | bytes 1572872 | tf_op jit(solution)/shard_map/ppermute | solution.py:30
  22.1 72.0 %collective-permute-start.12 = (bf16[11776,128]{1,0:T(8,128)(2,1)}, bf16[11776,128]{1,0:T(8,128)(2,1)S(1)}, u32[]{:S(2)}, u32[]{:S(2)}) collective-permute-start(bf16[11776,128]{1,0:T(8,128)(2,1)} %copy-done.3), channel_id=1, source_target_pairs={{0,24},{8,16},{16,8},{24,0},{1,25},{9,17},{17,9},{25,1},{2,26},{10... | collective-permute-start | bytes 9043976 | tf_op jit(solution)/shard_map/ppermute | solution.py:30
  24.5 16.7 %collective-permute-start.5 = (bf16[2048,128]{1,0:T(8,128)(2,1)S(1)}, bf16[2048,128]{1,0:T(8,128)(2,1)S(1)}, u32[]{:S(2)}, u32[]{:S(2)}) collective-permute-start(bf16[2048,128]{1,0:T(8,128)(2,1)S(1)} %collective-permute-done.4.refs_1_.refs_0_), channel_id=1, source_target_pairs={{0,2},{1,3},{2,4},{3,5},{4,6},{5,7},{6,0},{7,1},{8,10},{9,11},{10,... | collective-permute-start | bytes 1572872 | tf_op jit(solution)/shard_map/ppermute | solution.py:40
  29.6 31.5 %collective-permute-start.3 = (bf16[3600,128]{1,0:T(8,128)(2,1)}, bf16[3600,128]{1,0:T(8,128)(2,1)}, u32[]{:S(2)}, u32[]{:S(2)}) collective-permute-start(bf16[3600,128]{1,0:T(8,128)(2,1)} %hold.8.refs_2_), channel_id=1, source_target_pairs={{0,2},{1,3},{2,4},{3,5},{4,6},{5,7},{6,0},{7,1},{8,10},{9,11},{10,... | collective-permute-start | bytes 2764808 | tf_op jit(solution)/shard_map/ppermute | solution.py:40
  41.2 29.6 %collective-permute-start.9 = (bf16[2048,128]{1,0:T(8,128)(2,1)S(1)}, bf16[2048,128]{1,0:T(8,128)(2,1)S(1)}, u32[]{:S(2)}, u32[]{:S(2)}) collective-permute-start(bf16[2048,128]{1,0:T(8,128)(2,1)S(1)} %collective-permute-done.5.refs_1_.refs_2_), channel_id=1, source_target_pairs={{0,2},{1,3},{2,4},{3,5},{4,6},{5,7},{6,0},{7,1},{8,10},{9,11},{10,... | collective-permute-start | bytes 1572872 | tf_op jit(solution)/shard_map/ppermute | solution.py:40
  41.2 29.7 %collective-permute-start = (bf16[3600,128]{1,0:T(8,128)(2,1)}, bf16[3600,128]{1,0:T(8,128)(2,1)}, u32[]{:S(2)}, u32[]{:S(2)}) collective-permute-start(bf16[3600,128]{1,0:T(8,128)(2,1)} %get-tuple-element.33.refs_0_), channel_id=1, source_target_pairs={{0,1},{1,0},{2,3},{3,2},{4,5},{5,4},{6,7},{7,6},{8,9},{9,8},{10,11... | collective-permute-start | bytes 2764808 | tf_op jit(solution)/shard_map/ppermute | solution.py:35
  41.2 29.7 %collective-permute-start.2 = (bf16[3600,128]{1,0:T(8,128)(2,1)}, bf16[3600,128]{1,0:T(8,128)(2,1)}, u32[]{:S(2)}, u32[]{:S(2)}) collective-permute-start(bf16[3600,128]{1,0:T(8,128)(2,1)} %hold.8.refs_2_), channel_id=1, source_target_pairs={{0,1},{1,0},{2,3},{3,2},{4,5},{5,4},{6,7},{7,6},{8,9},{9,8},{10,11... | collective-permute-start | bytes 2764808 | tf_op jit(solution)/shard_map/ppermute | solution.py:35
  61.0 9.9 %collective-permute-start.6 = (bf16[3600,128]{1,0:T(8,128)(2,1)}, bf16[3600,128]{1,0:T(8,128)(2,1)}, u32[]{:S(2)}, u32[]{:S(2)}) collective-permute-start(bf16[3600,128]{1,0:T(8,128)(2,1)} %hold.9.refs_4_.refs_1_), channel_id=1, source_target_pairs={{0,1},{1,0},{2,3},{3,2},{4,5},{5,4},{6,7},{7,6},{8,9},{9,8},{10,11... | collective-permute-start | bytes 2764808 | tf_op jit(solution)/shard_map/ppermute | solution.py:35
  70.8 23.2 %collective-permute-start.8 = (bf16[3600,128]{1,0:T(8,128)(2,1)}, bf16[3600,128]{1,0:T(8,128)(2,1)}, u32[]{:S(2)}, u32[]{:S(2)}) collective-permute-start(bf16[3600,128]{1,0:T(8,128)(2,1)} %hold.9.refs_4_.refs_1_), channel_id=1, source_target_pairs={{0,2},{1,3},{2,4},{3,5},{4,6},{5,7},{6,0},{7,1},{8,10},{9,11},{10,... | collective-permute-start | bytes 2764808 | tf_op jit(solution)/shard_map/ppermute | solution.py:40
  94.1 2.7 %collective-permute-start.10 = (bf16[3600,128]{1,0:T(8,128)(2,1)}, bf16[3600,128]{1,0:T(8,128)(2,1)S(1)}, u32[]{:S(2)}, u32[]{:S(2)}) collective-permute-start(bf16[3600,128]{1,0:T(8,128)(2,1)} %hold.11.refs_0_), channel_id=1, source_target_pairs={{0,1},{1,0},{2,3},{3,2},{4,5},{5,4},{6,7},{7,6},{8,9},{9,8},{10,11... | collective-permute-start | bytes 2764808 | tf_op jit(solution)/shard_map/ppermute | solution.py:35
  94.1 13.8 %collective-permute-start.13 = (bf16[1536,128]{1,0:T(8,128)(2,1)S(1)}, bf16[1536,128]{1,0:T(8,128)(2,1)S(1)}, u32[]{:S(2)}, u32[]{:S(2)}) collective-permute-start(bf16[1536,128]{1,0:T(8,128)(2,1)S(1)} %top_rows.1.refs_0_), channel_id=1, source_target_pairs={{0,2},{1,3},{2,4},{3,5},{4,6},{5,7},{6,0},{7,1},{8,10},{9,11},{10,... | collective-permute-start | bytes 1179656 | tf_op jit(solution)/shard_map/ppermute | solution.py:40
  94.2 24.9 %collective-permute-start.19 = (bf16[2048,128]{1,0:T(8,128)(2,1)S(1)}, bf16[2048,128]{1,0:T(8,128)(2,1)S(1)}, u32[]{:S(2)}, u32[]{:S(2)}) collective-permute-start(bf16[2048,128]{1,0:T(8,128)(2,1)S(1)} %hold.10.refs_1_.refs_0_.refs_4_), channel_id=1, source_target_pairs={{0,2},{1,3},{2,4},{3,5},{4,6},{5,7},{6,0},{7,1},{8,10},{9,11},{10,... | collective-permute-start | bytes 1572872 | tf_op jit(solution)/shard_map/ppermute | solution.py:40
  94.2 24.9 %collective-permute-start.16 = (bf16[2048,128]{1,0:T(8,128)(2,1)S(1)}, bf16[2048,128]{1,0:T(8,128)(2,1)S(1)}, u32[]{:S(2)}, u32[]{:S(2)}) collective-permute-start(bf16[2048,128]{1,0:T(8,128)(2,1)S(1)} %copy-done.5), channel_id=1, source_target_pairs={{0,1},{1,0},{2,3},{3,2},{4,5},{5,4},{6,7},{7,6},{8,9},{9,8},{10,11... | collective-permute-start | bytes 1572872 | tf_op jit(solution)/shard_map/ppermute | solution.py:35
  94.8 27.1 %collective-permute-start.17 = (bf16[2048,128]{1,0:T(8,128)(2,1)S(1)}, bf16[2048,128]{1,0:T(8,128)(2,1)S(1)}, u32[]{:S(2)}, u32[]{:S(2)}) collective-permute-start(bf16[2048,128]{1,0:T(8,128)(2,1)S(1)} %copy-done.7), channel_id=1, source_target_pairs={{0,1},{1,0},{2,3},{3,2},{4,5},{5,4},{6,7},{7,6},{8,9},{9,8},{10,11... | collective-permute-start | bytes 1572872 | tf_op jit(solution)/shard_map/ppermute | solution.py:35
  96.8 25.3 %collective-permute-start.18 = (bf16[2048,128]{1,0:T(8,128)(2,1)S(1)}, bf16[2048,128]{1,0:T(8,128)(2,1)S(1)}, u32[]{:S(2)}, u32[]{:S(2)}) collective-permute-start(bf16[2048,128]{1,0:T(8,128)(2,1)S(1)} %hold.10.refs_1_.refs_0_.refs_4_), channel_id=1, source_target_pairs={{0,1},{1,0},{2,3},{3,2},{4,5},{5,4},{6,7},{7,6},{8,9},{9,8},{10,11... | collective-permute-start | bytes 1572872 | tf_op jit(solution)/shard_map/ppermute | solution.py:35
  107.9 19.3 %collective-permute-start.14 = (bf16[1536,128]{1,0:T(8,128)(2,1)S(1)}, bf16[1536,128]{1,0:T(8,128)(2,1)S(1)}, u32[]{:S(2)}, u32[]{:S(2)}) collective-permute-start(bf16[1536,128]{1,0:T(8,128)(2,1)S(1)} %hold.13.refs_1_.refs_2_), channel_id=1, source_target_pairs={{0,2},{1,3},{2,4},{3,5},{4,6},{5,7},{6,0},{7,1},{8,10},{9,11},{10,... | collective-permute-start | bytes 1179656 | tf_op jit(solution)/shard_map/ppermute | solution.py:40
  119.1 9.3 %collective-permute-start.20 = (bf16[2048,128]{1,0:T(8,128)(2,1)S(1)}, bf16[2048,128]{1,0:T(8,128)(2,1)S(1)}, u32[]{:S(2)}, u32[]{:S(2)}) collective-permute-start(bf16[2048,128]{1,0:T(8,128)(2,1)S(1)} %hold.14.refs_6_), channel_id=1, source_target_pairs={{0,1},{1,0},{2,3},{3,2},{4,5},{5,4},{6,7},{7,6},{8,9},{9,8},{10,11... | collective-permute-start | bytes 1572872 | tf_op jit(solution)/shard_map/ppermute | solution.py:35
  119.1 4.8 %collective-permute-start.7 = (f32[8,768]{1,0:T(8,128)S(1)}, f32[8,768]{1,0:T(8,128)S(1)}, u32[]{:S(2)}, u32[]{:S(2)}) collective-permute-start(f32[8,768]{1,0:T(8,128)S(1)} %get-tuple-element.36), channel_id=1, source_target_pairs={{0,24},{8,16},{16,8},{24,0},{1,25},{9,17},{17,9},{25,1},{2,26},{10... | collective-permute-start | bytes 73736 | tf_op jit(solution)/shard_map/ppermute | solution.py:30
  121.9 5.3 %collective-permute-start.11 = (f32[8,256]{1,0:T(8,128)S(1)}, f32[8,256]{1,0:T(8,128)S(1)}, u32[]{:S(2)}, u32[]{:S(2)}) collective-permute-start(f32[8,256]{1,0:T(8,128)S(1)} %get-tuple-element.40), channel_id=1, source_target_pairs={{0,24},{8,16},{16,8},{24,0},{1,25},{9,17},{17,9},{25,1},{2,26},{10... | collective-permute-start | bytes 24584 | tf_op jit(solution)/shard_map/ppermute | solution.py:30
  122.1 14.0 %collective-permute-start.21 = (bf16[1536,128]{1,0:T(8,128)(2,1)S(1)}, bf16[1536,128]{1,0:T(8,128)(2,1)S(1)}, u32[]{:S(2)}, u32[]{:S(2)}) collective-permute-start(bf16[1536,128]{1,0:T(8,128)(2,1)S(1)} %top_rows.1.refs_0_), channel_id=1, source_target_pairs={{0,1},{1,0},{2,3},{3,2},{4,5},{5,4},{6,7},{7,6},{8,9},{9,8},{10,11... | collective-permute-start | bytes 1179656 | tf_op jit(solution)/shard_map/ppermute | solution.py:35
  123.9 12.2 %collective-permute-start.22 = (bf16[1536,128]{1,0:T(8,128)(2,1)S(1)}, bf16[1536,128]{1,0:T(8,128)(2,1)S(1)}, u32[]{:S(2)}, u32[]{:S(2)}) collective-permute-start(bf16[1536,128]{1,0:T(8,128)(2,1)S(1)} %hold.13.refs_1_.refs_2_), channel_id=1, source_target_pairs={{0,1},{1,0},{2,3},{3,2},{4,5},{5,4},{6,7},{7,6},{8,9},{9,8},{10,11... | collective-permute-start | bytes 1179656 | tf_op jit(solution)/shard_map/ppermute | solution.py:35
  127.1 8.9 %collective-permute-start.23 = (bf16[1536,128]{1,0:T(8,128)(2,1)S(1)}, bf16[1536,128]{1,0:T(8,128)(2,1)S(1)}, u32[]{:S(2)}, u32[]{:S(2)}) collective-permute-start(bf16[1536,128]{1,0:T(8,128)(2,1)S(1)} %collective-permute-done.14.refs_4_), channel_id=1, source_target_pairs={{0,1},{1,0},{2,3},{3,2},{4,5},{5,4},{6,7},{7,6},{8,9},{9,8},{10,11... | collective-permute-start | bytes 1179656 | tf_op jit(solution)/shard_map/ppermute | solution.py:35
  127.1 13.3 %collective-permute-start.15 = (bf16[1536,128]{1,0:T(8,128)(2,1)S(1)}, bf16[1536,128]{1,0:T(8,128)(2,1)S(1)}, u32[]{:S(2)}, u32[]{:S(2)}) collective-permute-start(bf16[1536,128]{1,0:T(8,128)(2,1)S(1)} %collective-permute-done.14.refs_4_), channel_id=1, source_target_pairs={{0,2},{1,3},{2,4},{3,5},{4,6},{5,7},{6,0},{7,1},{8,10},{9,11},{10,... | collective-permute-start | bytes 1179656 | tf_op jit(solution)/shard_map/ppermute | solution.py:40
  (10 other events, 86.5 us)
